TPU v7x, 32 devices: a whole 2x2x4 slice. The times are simulated.
32 devices in a mesh: groups: 2 (over x), mp: 16 (over z, y, core).
Axes of the slice: x: 2, y: 2, z: 4, core: 2. Of those that a mesh axis runs over, the one named last changes fastest.
Arguments:
- acts: bfloat16 [8, 8192, 512], P('groups', 'mp'), parts along dimension 0, may hold values from -6 to 6
- output_gradients: bfloat16 [8, 8192, 512], P('groups', 'mp'), parts along dimension 0, may hold values from -6 to 6
- adapter_down: bfloat16 [128, 8192], P(None, 'mp'), may hold values from -0.0625 to 0.0625
- adapter_up: bfloat16 [8192, 128], P('mp'), may hold values from -0.0625 to 0.0625
- lengths: int32 [8], P('groups'), parts along dimension 0, may hold values from 128 to 512, as said below
- sign_hash_seed: int32 [1], replicated, may hold values from 0 to 1073741823
- tile_indices: int32 [8192], P('mp'), may hold values from 0 to 8191, each once
- validation_projected: float32 [512, 8192], P('groups', 'mp'), parts along dimension 0, may hold values from -6 to 6
Outputs:
- unit_grads: float32 [8, 8192], P('groups', 'mp'), parts along dimension 0
- alignment: float32 [8, 256], P('groups'), parts along dimension 0
- task_score: float32 [8, 4], P('groups'), parts along dimension 0
There are 2 independent parts, one for each index of `groups`. A program takes and returns all parts, laid end to end along the dimension named above; an argument that names none is the same for every part. Nothing has to cross between parts.
Inputs may be any that keep to these rules, and one draw needn't show every extreme that they name: `lengths`: every example keeps a quarter of 512 or more tokens; one example of every group is full length. `tile_indices`: a permutation of the row numbers.
All inputs are finite; a program needn't handle non-finite values.
Results may differ from a plain program's by a relative error of at most 0.0046.
Values may be sent and summed in bfloat16 or wider, within the bound.
No kernel may reach another device: no remote copies, remote signals or barrier semaphores. Data moves between devices by JAX's collectives and lax.ppermute only.
A program may use at most 64 MiB of HBM per device.

v0:
```python
import math

import jax
import jax.numpy as jnp
from jax import lax
from jax.sharding import PartitionSpec as P

PROJECTED_DIMS = 8192
TASKS = 4


def scramble(hashed):
    hashed = hashed ^ lax.shift_right_logical(hashed, jnp.full_like(hashed, 16))
    hashed = hashed * jnp.int32(2146121005)
    hashed = hashed ^ lax.shift_right_logical(hashed, jnp.full_like(hashed, 15))
    hashed = hashed * jnp.int32(-2073254261)
    hashed = hashed ^ lax.shift_right_logical(hashed, jnp.full_like(hashed, 16))
    return hashed


def sign_block(block_seeds, projected_begin, projected_count, span_width):
    groups = span_width // 32
    count_of_rows = block_seeds.shape[0]
    group_ids = lax.broadcasted_iota(jnp.int32, (1, groups, projected_count), 1)
    columns = lax.broadcasted_iota(jnp.int32, (1, groups, projected_count), 2) + projected_begin
    hash_words = scramble(block_seeds[:, None, None] + group_ids * PROJECTED_DIMS + columns)
    shifts = lax.broadcasted_iota(jnp.int32, (count_of_rows, groups, 32, projected_count), 2)
    spread = jnp.broadcast_to(
        hash_words[:, :, None, :], (count_of_rows, groups, 32, projected_count)
    )
    bit_values = lax.shift_right_logical(spread, shifts) & 1
    sign_tile = (1.0 - 2.0 * bit_values.astype(jnp.float32)).astype(jnp.bfloat16)
    return sign_tile.reshape(count_of_rows, span_width, projected_count)


def project_gradient(adapter_gradients, seeds_per_row, projected_begin, projected_count):
    count_of_rows = adapter_gradients.shape[1]
    span_width = adapter_gradients.shape[2]
    block_of_rows = math.gcd(count_of_rows, 4)

    def add_block(step_index, running):
        leading_row = step_index * block_of_rows
        block_seeds = lax.dynamic_slice_in_dim(seeds_per_row, leading_row, block_of_rows, 0)
        gradient_portion = lax.dynamic_slice_in_dim(
            adapter_gradients, leading_row, block_of_rows, 1
        )
        sign_tile = sign_block(block_seeds, projected_begin, projected_count, span_width)
        return running + jnp.einsum(
            "iwk,eiw->ke", sign_tile, gradient_portion, preferred_element_type=jnp.float32
        )

    initial_value = jnp.zeros((projected_count, adapter_gradients.shape[0]), jnp.float32)
    return lax.fori_loop(0, count_of_rows // block_of_rows, add_block, initial_value)


def shards(
    acts,
    output_gradients,
    adapter_down,
    adapter_up,
    lengths,
    sign_hash_seed,
    tile_indices,
    validation_projected,
):
    examples, local_width, seq_len = acts.shape
    positions = lax.broadcasted_iota(jnp.int32, (examples, seq_len), 1)
    live_mask = positions < lengths[:, None]
    masked_values = jnp.where(
        live_mask[:, None, :], output_gradients, jnp.zeros_like(output_gradients)
    )
    outgoing_total = jnp.einsum(
        "vwx,wi->vxi", masked_values, adapter_up, preferred_element_type=jnp.float32
    )
    incoming_total = jnp.einsum(
        "mwx,tw->mxt", acts, adapter_down, preferred_element_type=jnp.float32
    )
    local_terms = jnp.concatenate([outgoing_total, incoming_total], 2).reshape(
        examples * seq_len, -1
    )
    summed = lax.psum_scatter(local_terms, "mp", scatter_dimension=0, tiled=True)
    hidden_state = lax.all_gather(summed.astype(jnp.bfloat16), "mp", axis=0, tiled=True).reshape(
        examples, seq_len, -1
    )
    adapter_rank = adapter_down.shape[0]
    down_gradient = jnp.einsum(
        "xqf,xfk->xqk", acts, hidden_state[:, :, :adapter_rank], preferred_element_type=jnp.float32
    )
    up_gradient = jnp.einsum(
        "xqf,xfk->xqk",
        masked_values,
        hidden_state[:, :, adapter_rank:],
        preferred_element_type=jnp.float32,
    )
    adapter_gradients = jnp.concatenate([down_gradient, up_gradient], 2).astype(jnp.bfloat16)
    seeds_per_row = scramble(tile_indices + scramble(sign_hash_seed[0]))
    local_k = validation_projected.shape[1]
    nearby_projection = project_gradient(adapter_gradients, seeds_per_row, 0, PROJECTED_DIMS)
    whole_proj = lax.psum(nearby_projection, "mp")
    validation = lax.all_gather(validation_projected, "mp", axis=1, tiled=True)
    train_sq = jnp.sum(whole_proj * whole_proj, 0)
    val_sq = jnp.sum(validation * validation, 1)
    inner_products = jnp.einsum(
        "ke,vk->ev", whole_proj, validation, precision=lax.Precision.HIGHEST
    )
    own_rows = lax.dynamic_slice_in_dim(whole_proj, lax.axis_index("mp") * local_k, local_k, 0)
    train_norm = jnp.sqrt(train_sq + 1e-06)
    val_norm = jnp.sqrt(val_sq + 1e-06)
    factor = math.sqrt(PROJECTED_DIMS)
    unit_grads = (own_rows * (factor / train_norm)[None, :]).T
    alignment = factor * inner_products / (train_norm[:, None] * val_norm[None, :])
    task_score = jnp.mean(alignment.reshape(examples, TASKS, -1), 2)
    return (unit_grads, alignment, task_score)


def solution(mesh):
    placed = (
        P("groups", "mp", None),
        P("groups", "mp", None),
        P(None, "mp"),
        P("mp", None),
        P("groups"),
        P(),
        P("mp"),
        P("groups", "mp"),
    )
    return jax.shard_map(
        shards,
        mesh=mesh,
        in_specs=placed,
        out_specs=(P("groups", "mp"), P("groups", None), P("groups", None)),
        check_vma=False,
    )
```

profile of v0, /device:TPU:0, one launch (start us, length us, event | category | flops | bytes accessed | tf_op | source)
XLA Modules:
  0.0 2447.1 jit_solution(6410509532207700156)
XLA Ops:
  15.1 64.4 %reduce-scatter.2.cloned.1.call-done = f32[128,256]{1,0:T(8,128)} async-done(((f32[2048,256]{1,0:T(8,128)}), f32[128,256]{1,0:T(8,128)}) %reduce-scatter.2.cloned.1.call-update) | async-done | bytes 131088 | tf_op jit(solution)/shard_map/reduce_scatter | solution.py:81
  81.8 37.1 %all-gather.3.cloned.1.call-done = bf16[2048,256]{1,0:T(8,128)(2,1)} async-done(((bf16[128,256]{1,0:T(8,128)(2,1)}), bf16[2048,256]{1,0:T(8,128)(2,1)}) %all-gather.3.cloned.1.call-update) | async-done | bytes 1048592 | tf_op jit(solution)/shard_map/all_gather | solution.py:82
  123.8 2138.1 %while.14 = (s32[]{:T(128)}, f32[8192,4]{0,1:T(4,128)S(1)}, s32[512]{0:T(512)S(1)}, bf16[4,512,256]{2,0,1:T(4,128)(2,1)}, s32[]{:T(128)}, /*index=5*/s32[]{:T(128)}, s32[]{:T(128)}, s32[]{:T(128)}) while((s32[]{:T(128)}, f32[8192,4]{0,1:T(4,128)S(1)}, s32[512]{0:T(512)S(1)}, bf16[4,512,256]{2,0,1:T(4,128)(2,1)}, s32[]{:T(128)}, ...), condition=%wide.region_2.3_spmd.clone, body=%wide.region_1.2_spmd.clone.sunk | while | flops 120127504 | bytes 35926276 | solution.py:53
  124.4 8.1 fusion.37
  141.1 8.1 fusion.37
  157.8 8.1 fusion.37
  174.5 8.1 fusion.37
  191.2 8.1 fusion.37
  207.9 8.1 fusion.37
  224.6 8.1 fusion.37
  241.3 8.1 fusion.37
  258.0 8.1 fusion.37
  274.7 8.1 fusion.37
  291.4 8.1 fusion.37
  308.1 8.1 fusion.37
  324.8 8.1 fusion.37
  341.5 8.1 fusion.37
  358.2 8.1 fusion.37
  374.9 8.1 fusion.37
  391.6 8.1 fusion.37
  408.3 8.1 fusion.37
  425.0 8.1 fusion.37
  441.7 8.1 fusion.37
  458.4 8.1 fusion.37
  475.1 8.1 fusion.37
  491.8 8.1 fusion.37
  508.5 8.1 fusion.37
  525.3 8.1 fusion.37
  542.0 8.1 fusion.37
  558.7 8.1 fusion.37
  575.4 8.1 fusion.37
  592.1 8.1 fusion.37
  608.8 8.1 fusion.37
  625.5 8.1 fusion.37
  642.2 8.1 fusion.37
  658.9 8.1 fusion.37
  675.6 8.1 fusion.37
  692.3 8.1 fusion.37
  709.0 8.1 fusion.37
  725.7 8.1 fusion.37
  742.4 8.1 fusion.37
  759.1 8.1 fusion.37
  775.8 8.1 fusion.37
  792.5 8.1 fusion.37
  876.0 8.1 fusion.37
  959.5 8.1 fusion.37
  1043.1 8.1 fusion.37
  1109.9 8.1 fusion.37
  1193.4 8.1 fusion.37
  1276.9 8.1 fusion.37
  1360.4 8.1 fusion.37
  1427.2 8.1 fusion.37
  1510.8 8.1 fusion.37
  1594.3 8.1 fusion.37
  1677.8 8.1 fusion.37
  1744.6 8.1 fusion.37
  1828.1 8.1 fusion.37
  1911.7 8.1 fusion.37
  1995.2 8.1 fusion.37
  2062.0 8.1 fusion.37
  2145.5 8.1 fusion.37
  2229.0 8.1 fusion.37
  2263.1 85.4 %all-reduce.2.cloned.1.call-done = f32[8192,4]{0,1:T(4,128)} async-done(((f32[8192,4]{0,1:T(4,128)}), f32[8192,4]{0,1:T(4,128)}) %all-reduce.2.cloned.1.call-update) | async-done | bytes 131088 | tf_op jit(solution)/shard_map/psum | solution.py:99
  2351.1 76.3 %all-gather.5.cloned.1.call-done = f32[256,8192]{1,0:T(8,128)} async-done(((f32[256,512]{1,0:T(8,128)}), f32[256,8192]{1,0:T(8,128)}) %all-gather.5.cloned.1.call-update) | async-done | bytes 8388624 | tf_op jit(solution)/shard_map/all_gather | solution.py:100
  (884 shorter events, 1690.8 us)
Async XLA Ops:
  7.2 1.6 copy-start
  7.2 3.0 copy-start.8
  7.2 72.3 %reduce-scatter.2.cloned.1.call-start = ((), (), s32[]{:S(2)}) async-start(), calls=%async_computation.1 | async-start | bytes 2228224 | tf_op jit(solution)/shard_map/reduce_scatter | solution.py:81
  7.2 2.9 copy-start.7
  15.1 66.7 %copy-start.6 = (s32[512]{0:T(512)S(1)}, s32[512]{0:T(512)}, u32[]{:S(2)}) copy-start(s32[512]{0:T(512)} %param.16) | copy-start | bytes 6148
  15.1 103.8 %all-gather.3.cloned.1.call-start = ((), (), s32[]{:S(2)}) async-start(), calls=%async_computation.2 | async-start | bytes 1114112 | tf_op jit(solution)/shard_map/all_gather | solution.py:82
  81.1 2267.5 %all-reduce.2.cloned.1.call-start = ((), (), s32[]{:S(2)}) async-start(), calls=%async_computation.3 | async-start | bytes 262144 | tf_op jit(solution)/shard_map/psum | solution.py:99
  118.9 2.6 copy-start.4
  2261.9 0.7 copy-start.2
  2262.5 164.8 %all-gather.5.cloned.1.call-start = ((), (), s32[]{:S(2)}) async-start(), calls=%async_computation.4 | async-start | bytes 8912896 | tf_op jit(solution)/shard_map/all_gather | solution.py:100
  2348.5 83.1 %copy-start.3 = (f32[8192,4]{0,1:T(4,128)S(1)}, f32[8192,4]{0,1:T(4,128)}, u32[]{:S(2)}) copy-start(f32[8192,4]{0,1:T(4,128)} %all-reduce.2.cloned.1.call-done) | copy-start | bytes 393220
  2427.4 5.8 copy-start.1
  2439.7 0.8 copy-start.5
Sparse Core Ops, SparseCore 0:
  15.2 64.2 reduce-scatter.1
  81.9 36.9 all-gather.2
  2262.7 85.8 all-reduce.1
  2350.8 76.5 all-gather.4
where the time goes:
time: 2450 us
  other arithmetic  1100 us (45%)
  matrix products  1040 us (42%)
  waiting for transfers between devices  264 us (11%)
  local copies, waits for them, and re-layouts  27.5 us (1%)
    convert_element_type x128, other arithmetic, sign_block(): (1.0 - 2.0 * bit_values.astype(jnp.float32)).astype(jnp.bfloat16)  1030 us
    dot_general x128, matrix products, add_block(): jnp.einsum('iwk,eiw->ke', sign_tile, gradient_portion, preferred_element_...  1030 us
    psum x1, waiting for transfers between devices, shards(): whole_proj = lax.psum(nearby_projection, 'mp')  85.4 us
    all_gather x1, waiting for transfers between devices, shards(): validation = lax.all_gather(validation_projected, 'mp', axis=1, tiled=True)  76.3 us
    reduce_scatter x1, waiting for transfers between devices, shards(): lax.psum_scatter(local_terms, 'mp', scatter_dimension=0, tiled=True)  64.4 us
    xor x129, other arithmetic, scramble(): hashed = hashed ^ lax.shift_right_logical(hashed, jnp.full_like(hashed, 16))  49.9 us
  transfers between devices with their start and end apart: 4, of which 4 were waited for; matrix products, arithmetic and copies ran while one was open for 0% of the time, Pallas kernels for 0%

commit v1 on v0

v1 whole, which is shorter than its diff:
```python
import functools
import math

import jax
import jax.numpy as jnp
from jax import lax
from jax.experimental import pallas as pl
from jax.experimental.pallas import tpu as pltpu
from jax.sharding import PartitionSpec as P

PROJECTED_DIMS = 8192
TASKS = 4
DIGITS = 8
DIGIT_STEP = 16.0
DIGIT_TOP = 8.0
F8 = jnp.float8_e4m3fn
SPANS = ((0, 0, 64), (0, 64, 64), (1, 0, 128))


def scramble(hashed):
    hashed = hashed ^ lax.shift_right_logical(hashed, jnp.full_like(hashed, 16))
    hashed = hashed * jnp.int32(2146121005)
    hashed = hashed ^ lax.shift_right_logical(hashed, jnp.full_like(hashed, 15))
    hashed = hashed * jnp.int32(-2073254261)
    hashed = hashed ^ lax.shift_right_logical(hashed, jnp.full_like(hashed, 16))
    return hashed


def whole(shape):
    return pl.BlockSpec(shape, lambda *_: (0,) * len(shape))


def hidden_kernel(masked, lengths_ref, weight_ref, values_ref, *out_refs):
    example = pl.program_id(0)
    product = jnp.dot(weight_ref[...], values_ref[0], preferred_element_type=jnp.float32)
    if masked:
        positions = lax.broadcasted_iota(jnp.int32, product.shape, 1)
        product = jnp.where(positions < lengths_ref[example], product, 0.0)
    begin = 0
    for out_ref in out_refs:
        out_ref[0] = product[begin : begin + out_ref.shape[1]]
        begin += out_ref.shape[1]


def partial_hidden(values, weight, lengths, counts, masked):
    examples, width, tokens = values.shape
    return pl.pallas_call(
        functools.partial(hidden_kernel, masked),
        grid=(examples,),
        in_specs=[
            pl.BlockSpec(memory_space=pltpu.SMEM),
            whole(weight.shape),
            pl.BlockSpec((1, width, tokens), lambda e: (e, 0, 0)),
        ],
        out_specs=[pl.BlockSpec((1, n, tokens), lambda e: (e, 0, 0)) for n in counts],
        out_shape=[jax.ShapeDtypeStruct((examples, n, tokens), jnp.float32) for n in counts],
        name="partial_hidden",
    )(lengths, weight, values)


def grads_kernel(masked, lengths_ref, place_ref, hidden_ref, values_ref, own_ref, other_ref):
    example = pl.program_id(0)
    rows = own_ref.shape[2]
    hidden = hidden_ref[0]
    if masked:
        positions = lax.broadcasted_iota(jnp.int32, hidden.shape, 1)
        hidden = jnp.where(positions < lengths_ref[example], hidden, jnp.zeros_like(hidden))
    mine = place_ref[0]
    for out_ref, half in ((own_ref, mine), (other_ref, 1 - mine)):
        values = values_ref[0, pl.ds(pl.multiple_of(half * rows, rows), rows), :]
        out_ref[0] = lax.dot_general(
            hidden, values, (((1,), (1,)), ((), ())), preferred_element_type=jnp.float32
        ).astype(jnp.bfloat16)


def gradients(hidden, values, lengths, place, masked):
    examples, columns, tokens = hidden.shape
    width = values.shape[1]
    shape = (examples, columns, width // 2)
    return pl.pallas_call(
        functools.partial(grads_kernel, masked),
        grid=(examples,),
        in_specs=[
            pl.BlockSpec(memory_space=pltpu.SMEM),
            pl.BlockSpec(memory_space=pltpu.SMEM),
            pl.BlockSpec((1, columns, tokens), lambda e: (e, 0, 0)),
            pl.BlockSpec((1, width, tokens), lambda e: (e, 0, 0)),
        ],
        out_specs=[pl.BlockSpec((1,) + shape[1:], lambda e: (e, 0, 0))] * 2,
        out_shape=[jax.ShapeDtypeStruct(shape, jnp.bfloat16)] * 2,
        name="gradients",
    )(lengths, place, hidden, values)


def digits_kernel(place_ref, own_ref, other_ref, digits_ref, scale_ref, turned):
    first = place_ref[0] == 0
    own, other = own_ref[...].astype(jnp.float32), other_ref[...].astype(jnp.float32)
    examples = own.shape[0]
    for e in range(examples):
        turned[:, e, :] = jnp.where(first, own[e], other[e])
        turned[:, examples + e, :] = jnp.where(first, other[e], own[e])
    values = turned[...]
    largest = jnp.max(jnp.max(jnp.abs(values), axis=0), axis=1, keepdims=True)
    largest = jnp.maximum(largest, 1e-30)
    rest = values * (DIGIT_TOP / largest)[None]
    digits = []
    for _ in range(DIGITS):
        digit = jnp.round(rest)
        digits.append(digit)
        rest = (rest - digit) * DIGIT_STEP
    digits_ref[...] = jnp.concatenate(digits, axis=1).astype(F8)
    scale_ref[...] = largest * (1 / DIGIT_TOP)


def split_digits(own, received, place):
    examples, columns, rows = own.shape
    lines = 2 * examples
    return pl.pallas_call(
        digits_kernel,
        grid=(1,),
        in_specs=[pl.BlockSpec(memory_space=pltpu.SMEM), whole(own.shape), whole(own.shape)],
        out_specs=[whole((columns, DIGITS * lines, rows)), whole((lines, 1))],
        out_shape=[
            jax.ShapeDtypeStruct((columns, DIGITS * lines, rows), F8),
            jax.ShapeDtypeStruct((lines, 1), jnp.float32),
        ],
        scratch_shapes=[pltpu.VMEM((columns, lines, rows), jnp.float32)],
        compiler_params=pltpu.CompilerParams(vmem_limit_bytes=48 << 20),
        name="split_digits",
    )(place, own, received)


def project_kernel(first_group, seeds_ref, digits_ref, scale_ref, before_ref, out_ref, total):
    block, group = pl.program_id(0), pl.program_id(1)
    count = total.shape[1]
    rows = seeds_ref.shape[0]
    begin = (first_group + group) * PROJECTED_DIMS + block * count

    @pl.when(group == 0)
    def _():
        total[...] = jnp.zeros_like(total)

    columns = lax.broadcasted_iota(jnp.int32, (rows, count), 1)
    words = scramble((seeds_ref[...] + begin) + columns)
    signs = []
    for byte in range(4):
        shifted = lax.shift_right_logical(words, jnp.full_like(words, 8 * byte)) if byte else words
        shifted = shifted.astype(jnp.int8)
        for bit in range(8):
            mask = jnp.int8((1 << bit) - 256 * (bit == 7))
            signs.append(jnp.where((shifted & mask) != 0, F8(-1), F8(1)))
    digits = jnp.concatenate([digits_ref[c] for c in range(32)], axis=1)
    total[...] += jnp.dot(
        digits, jnp.concatenate(signs, axis=0), preferred_element_type=jnp.float32
    )

    @pl.when(group == pl.num_programs(1) - 1)
    def _():
        examples = out_ref.shape[0]
        added = total[(DIGITS - 1) * examples :, :]
        for digit in reversed(range(DIGITS - 1)):
            added = added * (1 / DIGIT_STEP) + total[digit * examples : (digit + 1) * examples, :]
        out_ref[...] = before_ref[...] + added * scale_ref[...]


def project(seeds, digits, scale, before, first_group):
    rows = seeds.shape[0]
    columns, lines, _ = digits.shape
    examples = scale.shape[0]
    count = 2048
    return pl.pallas_call(
        functools.partial(project_kernel, first_group),
        grid=(PROJECTED_DIMS // count, columns // 32),
        in_specs=[
            whole((rows, 1)),
            pl.BlockSpec((32, lines, rows), lambda k, g: (g, 0, 0)),
            whole((examples, 1)),
            pl.BlockSpec((examples, count), lambda k, g: (0, k)),
        ],
        out_specs=pl.BlockSpec((examples, count), lambda k, g: (0, k)),
        out_shape=jax.ShapeDtypeStruct((examples, PROJECTED_DIMS), jnp.float32),
        scratch_shapes=[pltpu.VMEM((lines, count), jnp.float32)],
        cost_estimate=pl.CostEstimate(
            flops=2 * 256 * columns * rows * PROJECTED_DIMS, bytes_accessed=digits.size, transcendentals=0
        ),
        compiler_params=pltpu.CompilerParams(vmem_limit_bytes=48 << 20),
        name="project",
    )(seeds, digits, scale, before)


def shards(
    acts,
    output_gradients,
    adapter_down,
    adapter_up,
    lengths,
    sign_hash_seed,
    tile_indices,
    validation_projected,
    parts=2,
    devices=16,
):
    examples, width, tokens = acts.shape
    group = lax.axis_index("groups")
    place = group.astype(jnp.int32).reshape(1)

    terms = {}
    for half, (values, weight) in enumerate(((output_gradients, adapter_up.T), (acts, adapter_down))):
        spans = [s for s in SPANS if s[0] == half]
        found = partial_hidden(values, weight, lengths, [s[2] for s in spans], half == 0)
        terms.update(zip(spans, found))

    row_seeds = scramble(tile_indices + scramble(sign_hash_seed[0]))
    row_seeds = lax.dynamic_slice_in_dim(row_seeds, group * (width // 2), width // 2, 0)[:, None]

    projected = jnp.zeros((parts * examples, PROJECTED_DIMS), jnp.float32)
    for span in SPANS:
        half, begin, count = span
        rows = examples * count // devices
        sent = terms[span].reshape(devices, rows, tokens)
        summed = lax.all_to_all(sent, "mp", 0, 0, tiled=True).sum(0).astype(jnp.bfloat16)
        hidden = lax.all_to_all(
            jnp.broadcast_to(summed[None], (devices, rows, tokens)), "mp", 0, 0, tiled=True
        ).reshape(examples, count, tokens)
        values = output_gradients if half else acts
        own, other = gradients(hidden, values, lengths, place, half == 1)
        received = lax.ppermute(other, "groups", [(0, 1), (1, 0)])
        digits, scale = split_digits(own, received, place)
        projected = project(row_seeds, digits, scale, projected, (half * adapter_down.shape[0] + begin) // 32)

    local_k = validation_projected.shape[1]
    sent = projected.reshape(parts, examples, devices, local_k).transpose(0, 2, 1, 3)
    sent = sent.reshape(parts * devices, examples, local_k)
    own = lax.all_to_all(sent, ("groups", "mp"), 0, 0, tiled=True).sum(0)

    inner = jnp.einsum("ek,vk->ev", own, validation_projected, precision=lax.Precision.HIGHEST)
    val_sq = jnp.sum(validation_projected * validation_projected, 1)
    train_sq = jnp.sum(own * own, 1)
    packed = jnp.concatenate(
        [inner, val_sq[None, :], jnp.pad(train_sq, (0, inner.shape[1] - examples))[None, :]], 0
    )
    packed = jnp.pad(packed, ((0, -packed.shape[0] % 8), (0, 0)))
    summed = lax.all_to_all(
        jnp.broadcast_to(packed[None], (devices,) + packed.shape), "mp", 0, 0, tiled=True
    ).sum(0)
    train_norm = jnp.sqrt(summed[examples + 1, :examples] + 1e-06)
    val_norm = jnp.sqrt(summed[examples] + 1e-06)
    factor = math.sqrt(PROJECTED_DIMS)
    unit_grads = own * (factor / train_norm)[:, None]
    alignment = factor * summed[:examples] / (train_norm[:, None] * val_norm[None, :])
    task_score = jnp.mean(alignment.reshape(examples, TASKS, -1), 2)
    return (unit_grads, alignment, task_score)


def solution(mesh):
    placed = (
        P("groups", "mp", None),
        P("groups", "mp", None),
        P(None, "mp"),
        P("mp", None),
        P("groups"),
        P(),
        P("mp"),
        P("groups", "mp"),
    )
    return jax.shard_map(
        functools.partial(shards, parts=mesh.shape["groups"], devices=mesh.shape["mp"]),
        mesh=mesh,
        in_specs=placed,
        out_specs=(P("groups", "mp"), P("groups", None), P("groups", None)),
        check_vma=False,
    )
```

time: 2450 us -> 253 us (0.10)
  other arithmetic: 1100 us -> 1.94 us
  matrix products: 1040 us -> 0.51 us
  waiting for transfers between devices: 264 us -> 51.1 us
  Pallas kernels: 0 us -> 126 us
  blocking collectives: 0 us -> 33.1 us
  starting transfers between devices: 0.34 us -> 30.9 us
    dot_general x133 -> x1, matrix products: 1040 us -> 0.51 us  [shards(): jnp.einsum('ek,vk->ev', own, validation_projected, precision=lax.Precisio...]
    convert_element_type x129 -> x0, other arithmetic: 1030 us -> none  [the longest x128 1030 us: sign_block(): (1.0 - 2.0 * bit_values.astype(jnp.float32)).astype(jnp.bfloat16)]
    pallas_call x0 -> x11, Pallas kernels: none -> 126 us  [the longest x3 101 us: project(): pl.pallas_call(functools.partial(project_kernel, first_group), grid=(PROJ...]
    all_gather x2 -> x0, waiting for transfers between devices: 113 us -> none  [the longest x1 76.3 us: shards(): validation = lax.all_gather(validation_projected, 'mp', axis=1, tiled=True)]
    psum x1 -> x0, waiting for transfers between devices: 85.4 us -> none  [shards(): whole_proj = lax.psum(nearby_projection, 'mp')]
    reduce_scatter x1 -> x0, waiting for transfers between devices: 64.4 us -> none  [shards(): lax.psum_scatter(local_terms, 'mp', scatter_dimension=0, tiled=True)]
    all_to_all x0 -> x6, waiting for transfers between devices: none -> 51.1 us  [the longest x2 25 us: shards(): lax.all_to_all(sent, 'mp', 0, 0, tiled=True).sum(0).astype(jnp.bfloat16)]
    xor x129 -> x1, other arithmetic: 49.9 us -> 0.01 us  [scramble(): hashed = hashed ^ lax.shift_right_logical(hashed, jnp.full_like(hashed, 16))]
  transfers between devices with their start and end apart: 4 -> 9, of which waited for: 4 -> 5; matrix products, arithmetic and copies ran while one was open for 0% -> 1% of each run, Pallas kernels for 0% -> 26%
where the time goes in v1:
time: 253 us; the launch traced here: 252 us
  Pallas kernels  126 us (50%)
  waiting for transfers between devices  51.1 us (20%)
  blocking collectives  33.1 us (13%)
  starting transfers between devices  30.9 us (12%)
  local copies, waits for them, and re-layouts  6.21 us (2%)
    pallas_call x3, Pallas kernels, project(): pl.pallas_call(functools.partial(project_kernel, first_group), grid=(PROJ...  101 us
    all_to_all x2, waiting for transfers between devices, shards(): lax.all_to_all(sent, 'mp', 0, 0, tiled=True).sum(0).astype(jnp.bfloat16)  25 us
    all_to_all x1, blocking collectives, shards(): lax.all_to_all(sent, 'mp', 0, 0, tiled=True).sum(0).astype(jnp.bfloat16)  21.9 us
    all_to_all x3, waiting for transfers between devices, shards(): lax.all_to_all(jnp.broadcast_to(summed[None], (devices, rows, tokens)), '...  16 us
    all_to_all x3, starting transfers between devices, shards(): lax.all_to_all(jnp.broadcast_to(summed[None], (devices, rows, tokens)), '...  14.4 us
    pallas_call x3, Pallas kernels, gradients(): pl.pallas_call(functools.partial(grads_kernel, masked), grid=(examples,),...  12.3 us
    all_to_all x1, blocking collectives, shards(): lax.all_to_all(jnp.broadcast_to(packed[None], (devices,) + packed.shape),...  11.3 us
    all_to_all x1, waiting for transfers between devices, shards(): own = lax.all_to_all(sent, ('groups', 'mp'), 0, 0, tiled=True).sum(0)  10.2 us
  transfers between devices with their start and end apart: 9, of which 5 were waited for; matrix products, arithmetic and copies ran while one was open for 1% of the time, Pallas kernels for 26%

profile of v1, /device:TPU:0, one launch (start us, length us, event | category | flops | bytes accessed | tf_op | source)
XLA Modules:
  0.0 251.6 jit_solution(2584863766588066784)
XLA Ops:
  0.6 1.7 copy.23
  2.3 4.0 %partial_hidden.3 = (f32[4,64,512]{2,1,0:T(8,128)}, f32[4,64,512]{2,1,0:T(8,128)}) custom-call(s32[4]{0:T(128)} %lengths_ref.9, bf16[128,512]{1,0:T(8,128)(2,1)} %bitcast.34, bf16[4,512,512]{2,1,0:T(8,128)(2,1)} %values_ref.7), custom_call_target="tpu_custom_call" | custom-call | tf_op jit(solution)/shard_map/partial_hidden/pallas_call | solution.py:47
  6.3 21.9 %all_to_all.40 = f32[16,16,512]{2,1,0:T(8,128)S(1)} all-to-all(f32[16,16,512]{2,1,0:T(8,128)} %bitcast.36), channel_id=1, replica_groups=mesh['groups'=2,'mp'=16] {'mp'}, dimensions={0} | all-to-all | bytes 1048576 | tf_op jit(solution)/shard_map/all_to_all | solution.py:221
  28.1 4.1 %all-to-all-start.2 = ((f32[16,16,512]{2,1,0:T(8,128)}), f32[16,16,512]{2,1,0:T(8,128)S(1)}, u32[]{:S(2)}, u32[]{:S(2)}) async-start(f32[16,16,512]{2,1,0:T(8,128)} %bitcast.35), calls=%async_computation.2 | async-start | bytes 1048576 | tf_op jit(solution)/shard_map/all_to_all | solution.py:221
  32.3 14.4 %all-to-all-done.2 = f32[16,16,512]{2,1,0:T(8,128)S(1)} async-done(((f32[16,16,512]{2,1,0:T(8,128)}), f32[16,16,512]{2,1,0:T(8,128)S(1)}, u32[]{:S(2)}, u32[]{:S(2)}) %all-to-all-start.2) | async-done | bytes 524320 | tf_op jit(solution)/shard_map/all_to_all | solution.py:221
  46.7 0.7 broadcast_in_dim.22
  47.4 4.1 %all-to-all-start.5 = ((bf16[16,16,512]{2,1,0:T(8,128)(2,1)}), bf16[16,16,512]{2,1,0:T(8,128)(2,1)S(1)}, u32[]{:S(2)}, u32[]{:S(2)}) async-start(bf16[16,16,512]{2,1,0:T(8,128)(2,1)} %broadcast_in_dim.22), calls=%async_computation.5 | async-start | bytes 524288 | tf_op jit(solution)/shard_map/all_to_all | solution.py:222
  51.6 10.0 %all-to-all-done.5 = bf16[16,16,512]{2,1,0:T(8,128)(2,1)S(1)} async-done(((bf16[16,16,512]{2,1,0:T(8,128)(2,1)}), bf16[16,16,512]{2,1,0:T(8,128)(2,1)S(1)}, u32[]{:S(2)}, u32[]{:S(2)}) %all-to-all-start.5) | async-done | bytes 262176 | tf_op jit(solution)/shard_map/all_to_all | solution.py:222
  61.6 0.0 copy-start.6
  61.6 0.8 broadcast_in_dim.21
  62.4 3.5 %all-to-all-start.3 = ((bf16[16,16,512]{2,1,0:T(8,128)(2,1)}), bf16[16,16,512]{2,1,0:T(8,128)(2,1)S(1)}, u32[]{:S(2)}, u32[]{:S(2)}) async-start(bf16[16,16,512]{2,1,0:T(8,128)(2,1)} %broadcast_in_dim.21), calls=%async_computation.3 | async-start | bytes 524288 | tf_op jit(solution)/shard_map/all_to_all | solution.py:222
  65.9 4.0 %partial_hidden.2 = f32[4,128,512]{2,1,0:T(8,128)} custom-call(s32[4]{0:T(128)} %lengths_ref.9, bf16[128,512]{1,0:T(8,128)(2,1)} %weight_ref.1, bf16[4,512,512]{2,1,0:T(8,128)(2,1)} %values_ref.9), custom_call_target="tpu_custom_call" | custom-call | tf_op jit(solution)/shard_map/partial_hidden/pallas_call | solution.py:47
  69.9 6.0 %all-to-all-done.3 = bf16[16,16,512]{2,1,0:T(8,128)(2,1)S(1)} async-done(((bf16[16,16,512]{2,1,0:T(8,128)(2,1)}), bf16[16,16,512]{2,1,0:T(8,128)(2,1)S(1)}, u32[]{:S(2)}, u32[]{:S(2)}) %all-to-all-start.3) | async-done | bytes 262176 | tf_op jit(solution)/shard_map/all_to_all | solution.py:222
  75.9 0.0 copy-start.5
  75.9 0.0 copy-start.8
  75.9 0.0 copy-done.6
  75.9 3.8 %all-to-all-start = ((f32[16,32,512]{2,1,0:T(8,128)}), f32[16,32,512]{2,1,0:T(8,128)S(1)}, u32[]{:S(2)}, u32[]{:S(2)}) async-start(f32[16,32,512]{2,1,0:T(8,128)} %bitcast.28), calls=%async_computation | async-start | bytes 2097152 | tf_op jit(solution)/shard_map/all_to_all | solution.py:221
  80.4 4.1 %gradients.5 = (bf16[4,64,256]{2,1,0:T(8,128)(2,1)}, bf16[4,64,256]{2,1,0:T(8,128)(2,1)}) custom-call(s32[4]{0:T(128)} %lengths_ref.9, s32[1]{0:T(128)} %bitcast.2.place_ref, bf16[4,64,512]{2,1,0:T(8,128)(2,1)} %bitcast.31, bf16[4,512,512]{2,1,0:T(8,128)(2,1)} %values_ref.9), custom_call_target="tpu_custom_call" | custom-call | tf_op jit(solution)/shard_map/gradients/pallas_call | solution.py:80
  84.4 0.0 copy-done.5
  84.4 0.0 copy-start.2
  84.4 1.6 collective-permute-start.2
  86.0 0.0 copy-done.8
  86.0 0.1 dynamic_slice.3
  86.1 0.1 copy.26.seeds_ref
  86.2 4.0 %gradients.4 = (bf16[4,64,256]{2,1,0:T(8,128)(2,1)}, bf16[4,64,256]{2,1,0:T(8,128)(2,1)}) custom-call(s32[4]{0:T(128)} %lengths_ref.9, s32[1]{0:T(128)} %bitcast.2.place_ref, bf16[4,64,512]{2,1,0:T(8,128)(2,1)} %bitcast.30, bf16[4,512,512]{2,1,0:T(8,128)(2,1)} %values_ref.9), custom_call_target="tpu_custom_call" | custom-call | tf_op jit(solution)/shard_map/gradients/pallas_call | solution.py:80
  90.3 0.5 collective-permute-start.1
  90.8 0.0 collective-permute-done.2.other_ref
  90.8 0.0 copy-done.2
  90.8 1.3 split_digits.5
  92.1 10.5 %all-to-all-done = f32[16,32,512]{2,1,0:T(8,128)S(1)} async-done(((f32[16,32,512]{2,1,0:T(8,128)}), f32[16,32,512]{2,1,0:T(8,128)S(1)}, u32[]{:S(2)}, u32[]{:S(2)}) %all-to-all-start) | async-done | bytes 1048608 | tf_op jit(solution)/shard_map/all_to_all | solution.py:221
  102.6 0.1 reduce_sum.72
  102.7 0.9 broadcast_in_dim.20
  103.5 6.8 %all-to-all-start.1 = ((bf16[16,32,512]{2,1,0:T(8,128)(2,1)}), bf16[16,32,512]{2,1,0:T(8,128)(2,1)S(1)}, u32[]{:S(2)}, u32[]{:S(2)}) async-start(bf16[16,32,512]{2,1,0:T(8,128)(2,1)} %broadcast_in_dim.20), calls=%async_computation.1 | async-start | bytes 1048576 | tf_op jit(solution)/shard_map/all_to_all | solution.py:222
  110.4 0.0 copy-start.1
  110.4 25.3 %project.3.before_ref = f32[8,8192]{1,0:T(8,128)S(1)} custom-call(s32[256,1]{1,0:T(8,128)S(1)} %copy.26.seeds_ref, f8e4m3fn[64,64,256]{2,1,0:T(32,128)(4,1)S(1)} %get-tuple-element.29.digits_ref, f32[8,1]{1,0:T(8,128)S(1)} %get-tuple-element.30.scale_ref, f32[8,8192]{1,0:T(8,128)S(1)} %broadcast_in_dim.23.before_ref), custom_call_target="tpu_custom_call" | custom-call | flops 68719476736 | bytes 1048576 | tf_op jit(solution)/shard_map/project/pallas_call | solution.py:171
  135.7 0.0 collective-permute-done.1.other_ref
  135.7 0.0 copy-done.1
  135.7 1.3 split_digits.4
  137.0 0.0 all-to-all-done.1
  137.0 0.0 copy-start.3
  137.0 0.8 copy-done.3
  137.8 4.2 %gradients.3 = (bf16[4,128,256]{2,1,0:T(8,128)(2,1)}, bf16[4,128,256]{2,1,0:T(8,128)(2,1)}) custom-call(s32[4]{0:T(128)} %lengths_ref.9, s32[1]{0:T(128)} %bitcast.2.place_ref, bf16[4,128,512]{2,1,0:T(8,128)(2,1)} %bitcast.29, bf16[4,512,512]{2,1,0:T(8,128)(2,1)} %values_ref.7), custom_call_target="tpu_custom_call" | custom-call | tf_op jit(solution)/shard_map/gradients/pallas_call | solution.py:80
  142.0 1.5 collective-permute-start
  143.5 25.2 %project.4.before_ref = f32[8,8192]{1,0:T(8,128)S(1)} custom-call(s32[256,1]{1,0:T(8,128)S(1)} %copy.26.seeds_ref, f8e4m3fn[64,64,256]{2,1,0:T(32,128)(4,1)S(1)} %get-tuple-element.24.digits_ref, f32[8,1]{1,0:T(8,128)S(1)} %get-tuple-element.25.scale_ref, f32[8,8192]{1,0:T(8,128)S(1)} %project.3.before_ref), custom_call_target="tpu_custom_call" | custom-call | flops 68719476736 | bytes 1048576 | tf_op jit(solution)/shard_map/project/pallas_call | solution.py:171
  168.8 0.0 collective-permute-done.other_ref
  168.8 0.0 copy-done
  168.8 2.6 %split_digits.3 = (f8e4m3fn[128,64,256]{2,1,0:T(32,128)(4,1)S(1)}, f32[8,1]{1,0:T(8,128)S(1)}) custom-call(s32[1]{0:T(128)} %bitcast.2.place_ref, bf16[4,128,256]{2,1,0:T(8,128)(2,1)S(1)} %copy-done, bf16[4,128,256]{2,1,0:T(8,128)(2,1)S(1)} %collective-permute-done.other_ref), custom_call_target="tpu_custom_call" | custom-call | tf_op jit(solution)/shard_map/split_digits/pallas_call | solution.py:118
  171.3 50.4 %project.5 = f32[8,8192]{1,0:T(8,128)S(1)} custom-call(s32[256,1]{1,0:T(8,128)S(1)} %copy.26.seeds_ref, f8e4m3fn[128,64,256]{2,1,0:T(32,128)(4,1)S(1)} %get-tuple-element.19.digits_ref, f32[8,1]{1,0:T(8,128)S(1)} %get-tuple-element.20.scale_ref, f32[8,8192]{1,0:T(8,128)S(1)} %project.4.before_ref), custom_call_target="tpu_custom_call" | custom-call | flops 137438953472 | bytes 2097152 | tf_op jit(solution)/shard_map/project/pallas_call | solution.py:171
  221.7 0.2 copy.29
  221.9 0.9 copy.28
  222.8 4.9 %all-to-all-start.6 = ((f32[32,4,512]{2,1,0:T(4,128)}), f32[32,4,512]{2,1,0:T(4,128)S(1)}, u32[]{:S(2)}, u32[]{:S(2)}) async-start(f32[32,4,512]{2,1,0:T(4,128)} %copy.28), calls=%async_computation.6 | async-start | bytes 524288 | tf_op jit(solution)/shard_map/all_to_all | solution.py:234
  227.7 0.0 copy-done.4
  227.8 0.1 multiply_reduce_fusion
  227.9 10.2 %all-to-all-done.6 = f32[32,4,512]{2,1,0:T(4,128)S(1)} async-done(((f32[32,4,512]{2,1,0:T(4,128)}), f32[32,4,512]{2,1,0:T(4,128)S(1)}, u32[]{:S(2)}, u32[]{:S(2)}) %all-to-all-start.6) | async-done | bytes 262176 | tf_op jit(solution)/shard_map/all_to_all | solution.py:234
  238.0 0.1 reduce_sum.75
  238.1 0.5 fusion.4
  238.6 0.1 multiply_reduce_fusion.1
  238.8 11.3 %all_to_all.41 = f32[16,8,256]{2,1,0:T(8,128)S(1)} all-to-all(f32[16,8,256]{2,1,0:T(8,128)S(1)} %broadcast_in_dim.50), channel_id=1, replica_groups=mesh['groups'=2,'mp'=16] {'mp'}, dimensions={0} | all-to-all | bytes 262144 | tf_op jit(solution)/shard_map/all_to_all | solution.py:243
  250.1 0.1 fusion
  250.2 0.1 reshape.72
  250.3 0.1 reduce_sum.79
  250.4 0.6 broadcast_multiply_fusion.1
  251.0 0.7 broadcast_multiply_fusion
  251.6 0.0 copy-done.7
  (14 shorter events, 0.2 us)
Async XLA Ops:
  28.1 18.6 %all-to-all-start.2 = ((f32[16,16,512]{2,1,0:T(8,128)}), f32[16,16,512]{2,1,0:T(8,128)S(1)}, u32[]{:S(2)}, u32[]{:S(2)}) async-start(f32[16,16,512]{2,1,0:T(8,128)} %bitcast.35), calls=%async_computation.2 | async-start | bytes 1048576 | tf_op jit(solution)/shard_map/all_to_all | solution.py:221
  47.4 14.2 %all-to-all-start.5 = ((bf16[16,16,512]{2,1,0:T(8,128)(2,1)}), bf16[16,16,512]{2,1,0:T(8,128)(2,1)S(1)}, u32[]{:S(2)}, u32[]{:S(2)}) async-start(bf16[16,16,512]{2,1,0:T(8,128)(2,1)} %broadcast_in_dim.22), calls=%async_computation.5 | async-start | bytes 524288 | tf_op jit(solution)/shard_map/all_to_all | solution.py:222
  61.6 14.3 %copy-start.6 = (bf16[16,16,512]{2,1,0:T(8,128)(2,1)}, bf16[16,16,512]{2,1,0:T(8,128)(2,1)S(1)}, u32[]{:S(2)}) copy-start(bf16[16,16,512]{2,1,0:T(8,128)(2,1)S(1)} %all-to-all-done.5) | copy-start | bytes 786436
  62.4 13.5 %all-to-all-start.3 = ((bf16[16,16,512]{2,1,0:T(8,128)(2,1)}), bf16[16,16,512]{2,1,0:T(8,128)(2,1)S(1)}, u32[]{:S(2)}, u32[]{:S(2)}) async-start(bf16[16,16,512]{2,1,0:T(8,128)(2,1)} %broadcast_in_dim.21), calls=%async_computation.3 | async-start | bytes 524288 | tf_op jit(solution)/shard_map/all_to_all | solution.py:222
  75.9 8.5 %copy-start.5 = (bf16[16,16,512]{2,1,0:T(8,128)(2,1)}, bf16[16,16,512]{2,1,0:T(8,128)(2,1)S(1)}, u32[]{:S(2)}) copy-start(bf16[16,16,512]{2,1,0:T(8,128)(2,1)S(1)} %all-to-all-done.3) | copy-start | bytes 786436
  75.9 10.1 %copy-start.8 = (s32[512]{0:T(512)S(1)}, s32[512]{0:T(512)}, u32[]{:S(2)}) copy-start(s32[512]{0:T(512)} %param.14) | copy-start | bytes 6148
  75.9 26.7 %all-to-all-start = ((f32[16,32,512]{2,1,0:T(8,128)}), f32[16,32,512]{2,1,0:T(8,128)S(1)}, u32[]{:S(2)}, u32[]{:S(2)}) async-start(f32[16,32,512]{2,1,0:T(8,128)} %bitcast.28), calls=%async_computation | async-start | bytes 2097152 | tf_op jit(solution)/shard_map/all_to_all | solution.py:221
  84.4 6.4 %copy-start.2 = (bf16[4,64,256]{2,1,0:T(8,128)(2,1)S(1)}, bf16[4,64,256]{2,1,0:T(8,128)(2,1)}, u32[]{:S(2)}) copy-start(bf16[4,64,256]{2,1,0:T(8,128)(2,1)} %get-tuple-element.27.own_ref) | copy-start | bytes 393220
  84.4 6.4 %collective-permute-start.2 = (bf16[4,64,256]{2,1,0:T(8,128)(2,1)}, bf16[4,64,256]{2,1,0:T(8,128)(2,1)S(1)}, u32[]{:S(2)}, u32[]{:S(2)}) collective-permute-start(bf16[4,64,256]{2,1,0:T(8,128)(2,1)} %get-tuple-element.28), channel_id=1, source_target_pairs={{0,16},{16,0},{1,17},{17,1},{2,18},{18,2},{3,19},{19,3},{4,20},{20... | collective-permute-start | bytes 393224 | tf_op jit(solution)/shard_map/ppermute | solution.py:227
  90.3 45.4 %collective-permute-start.1 = (bf16[4,64,256]{2,1,0:T(8,128)(2,1)}, bf16[4,64,256]{2,1,0:T(8,128)(2,1)S(1)}, u32[]{:S(2)}, u32[]{:S(2)}) collective-permute-start(bf16[4,64,256]{2,1,0:T(8,128)(2,1)} %get-tuple-element.23), channel_id=1, source_target_pairs={{0,16},{16,0},{1,17},{17,1},{2,18},{18,2},{3,19},{19,3},{4,20},{20... | collective-permute-start | bytes 393224 | tf_op jit(solution)/shard_map/ppermute | solution.py:227
  103.5 33.4 %all-to-all-start.1 = ((bf16[16,32,512]{2,1,0:T(8,128)(2,1)}), bf16[16,32,512]{2,1,0:T(8,128)(2,1)S(1)}, u32[]{:S(2)}, u32[]{:S(2)}) async-start(bf16[16,32,512]{2,1,0:T(8,128)(2,1)} %broadcast_in_dim.20), calls=%async_computation.1 | async-start | bytes 1048576 | tf_op jit(solution)/shard_map/all_to_all | solution.py:222
  110.4 25.3 %copy-start.1 = (bf16[4,64,256]{2,1,0:T(8,128)(2,1)S(1)}, bf16[4,64,256]{2,1,0:T(8,128)(2,1)}, u32[]{:S(2)}) copy-start(bf16[4,64,256]{2,1,0:T(8,128)(2,1)} %get-tuple-element.22.own_ref) | copy-start | bytes 393220
  137.0 0.8 copy-start.3
  142.0 26.8 %collective-permute-start = (bf16[4,128,256]{2,1,0:T(8,128)(2,1)}, bf16[4,128,256]{2,1,0:T(8,128)(2,1)S(1)}, u32[]{:S(2)}, u32[]{:S(2)}) collective-permute-start(bf16[4,128,256]{2,1,0:T(8,128)(2,1)} %get-tuple-element.18), channel_id=1, source_target_pairs={{0,16},{16,0},{1,17},{17,1},{2,18},{18,2},{3,19},{19,3},{4,20},{20... | collective-permute-start | bytes 786440 | tf_op jit(solution)/shard_map/ppermute | solution.py:227
  143.5 25.3 %copy-start = (bf16[4,128,256]{2,1,0:T(8,128)(2,1)S(1)}, bf16[4,128,256]{2,1,0:T(8,128)(2,1)}, u32[]{:S(2)}) copy-start(bf16[4,128,256]{2,1,0:T(8,128)(2,1)} %get-tuple-element.17.own_ref) | copy-start | bytes 786436
  221.7 6.0 %copy-start.4 = (f32[256,512]{1,0:T(8,128)S(1)}, f32[256,512]{1,0:T(8,128)}, u32[]{:S(2)}) copy-start(f32[256,512]{1,0:T(8,128)} %param.15) | copy-start | bytes 1572868
  222.8 15.2 %all-to-all-start.6 = ((f32[32,4,512]{2,1,0:T(4,128)}), f32[32,4,512]{2,1,0:T(4,128)S(1)}, u32[]{:S(2)}, u32[]{:S(2)}) async-start(f32[32,4,512]{2,1,0:T(4,128)} %copy.28), calls=%async_computation.6 | async-start | bytes 524288 | tf_op jit(solution)/shard_map/all_to_all | solution.py:234
  250.2 1.4 copy-start.7

commit v2 on v1

v2 whole, which is shorter than its diff:
```python
import functools
import math

import jax
import jax.numpy as jnp
from jax import lax
from jax.experimental import pallas as pl
from jax.experimental.pallas import tpu as pltpu
from jax.sharding import Mesh
from jax.sharding import PartitionSpec as P

PROJECTED_DIMS = 8192
TASKS = 4
DIGITS = 4
DIGIT_STEP = 16.0
DIGIT_TOP = 8.0
F8 = jnp.float8_e4m3fn
PROJECTED_BLOCK = 2048


def scramble(hashed):
    hashed = hashed ^ lax.shift_right_logical(hashed, jnp.full_like(hashed, 16))
    hashed = hashed * jnp.int32(2146121005)
    hashed = hashed ^ lax.shift_right_logical(hashed, jnp.full_like(hashed, 15))
    hashed = hashed * jnp.int32(-2073254261)
    hashed = hashed ^ lax.shift_right_logical(hashed, jnp.full_like(hashed, 16))
    return hashed


def whole(shape):
    return pl.BlockSpec(shape, lambda *_: (0,) * len(shape))


def after(value, earlier):
    return pl.pallas_call(
        lambda value_ref, earlier_ref, out_ref: None,
        in_specs=[pl.BlockSpec(memory_space=pl.ANY), whole(earlier.shape)],
        out_specs=pl.BlockSpec(memory_space=pl.ANY),
        out_shape=jax.ShapeDtypeStruct(value.shape, value.dtype),
        input_output_aliases={0: 0},
        grid=(1,),
        name="after",
    )(value, earlier)


def hidden_kernel(masked, weight_dim, order_ref, lengths_ref, weight_ref, values_ref, earlier_ref, sent_ref, kept_ref, done_ref):
    step = pl.program_id(0)
    product = lax.dot_general(
        weight_ref[...], values_ref[0], (((weight_dim,), (0,)), ((), ())), preferred_element_type=jnp.float32
    )
    if masked:
        positions = lax.broadcasted_iota(jnp.int32, product.shape, 1)
        product = jnp.where(positions < lengths_ref[order_ref[step]], product, 0.0)
    early = step < sent_ref.shape[0] * (pl.num_programs(0) // 2)

    @pl.when(early)
    def _():
        sent_ref[0] = product

    @pl.when(jnp.logical_not(early))
    def _():
        kept_ref[0] = product

    done_ref[...] = earlier_ref[...]


def partial_hidden(values, weight, lengths, order, masked, earlier):
    examples, width, tokens = values.shape
    weight_dim = 0 if masked else 1
    count = weight.shape[1 - weight_dim]
    half = examples // 2
    shape = jax.ShapeDtypeStruct((half, count, tokens), jnp.float32)
    return pl.pallas_call(
        functools.partial(hidden_kernel, masked, weight_dim),
        grid_spec=pltpu.PrefetchScalarGridSpec(
            num_scalar_prefetch=1,
            grid=(examples,),
            in_specs=[
                pl.BlockSpec(memory_space=pltpu.SMEM),
                whole(weight.shape),
                pl.BlockSpec((1, width, tokens), lambda e, order: (order[e], 0, 0)),
                whole(earlier.shape),
            ],
            out_specs=[
                pl.BlockSpec((1, count, tokens), lambda e, order: (jnp.minimum(e, half - 1), 0, 0)),
                pl.BlockSpec((1, count, tokens), lambda e, order: (jnp.maximum(e - half, 0), 0, 0)),
                whole(earlier.shape),
            ],
        ),
        out_shape=[shape, shape, jax.ShapeDtypeStruct(earlier.shape, earlier.dtype)],
        name="partial_hidden",
    )(order, lengths, weight, values, earlier)


def sum_kernel(length_ref, terms_ref, earlier_ref, out_ref, done_ref):
    done_ref[...] = earlier_ref[...]
    summed = terms_ref[0]
    for n in range(1, terms_ref.shape[0]):
        summed = summed + terms_ref[n]
    positions = lax.broadcasted_iota(jnp.int32, summed.shape, 1)
    summed = jnp.where(positions < length_ref[0], summed, 0.0).astype(jnp.bfloat16)
    for n in range(out_ref.shape[0]):
        out_ref[n] = summed


def sum_terms(terms, length, copies, earlier):
    return pl.pallas_call(
        sum_kernel,
        grid=(1,),
        in_specs=[pl.BlockSpec(memory_space=pltpu.SMEM), whole(terms.shape), whole(earlier.shape)],
        out_specs=[whole((copies,) + terms.shape[1:]), whole(earlier.shape)],
        out_shape=[
            jax.ShapeDtypeStruct((copies,) + terms.shape[1:], jnp.bfloat16),
            jax.ShapeDtypeStruct(earlier.shape, earlier.dtype),
        ],
        name="sum_terms",
    )(length, terms, earlier)


def digits_kernel(
    place_ref, near_ref, far_ref, own_ref, other_ref, earlier_ref, digits_ref, scale_ref, turned
):
    group, core = place_ref[0], place_ref[1]
    examples = own_ref.shape[0]
    half = examples // 2
    for e in range(2 * examples):
        g, example = e // examples, e % examples
        values = jnp.where(group == g, own_ref[example], other_ref[example])
        slot = g * half + example % half
        hidden = jnp.where(core == example // half, near_ref[slot], far_ref[slot])
        grads = lax.dot_general(
            hidden, values, (((1,), (1,)), ((), ())), preferred_element_type=jnp.float32
        )
        turned[:, e, :] = grads.astype(jnp.bfloat16).astype(jnp.float32)
    values = turned[...]
    largest = jnp.max(jnp.max(jnp.abs(values), axis=0), axis=1, keepdims=True)
    largest = jnp.maximum(largest, 1e-30)
    rest = values * (DIGIT_TOP / largest)[None]
    digits = []
    for _ in range(DIGITS):
        digit = jnp.round(rest)
        digits.append(digit)
        rest = (rest - digit) * DIGIT_STEP
    digits_ref[...] = jnp.concatenate(digits, axis=1).astype(F8)
    scale_ref[...] = largest * (1 / DIGIT_TOP)


def gradient_digits(near, far, values, other, place, earlier):
    columns = near.shape[1]
    examples, rows, tokens = other.shape
    lines = 2 * examples
    return pl.pallas_call(
        digits_kernel,
        grid_spec=pltpu.PrefetchScalarGridSpec(
            num_scalar_prefetch=1,
            grid=(1,),
            in_specs=[
                whole(near.shape),
                whole(near.shape),
                pl.BlockSpec(other.shape, lambda _, place: (0, place[0], 0)),
                whole(other.shape),
                whole(earlier.shape),
            ],
            out_specs=[whole((columns, DIGITS * lines, rows)), whole((lines, 1))],
            scratch_shapes=[pltpu.VMEM((columns, lines, rows), jnp.float32)],
        ),
        out_shape=[
            jax.ShapeDtypeStruct((columns, DIGITS * lines, rows), F8),
            jax.ShapeDtypeStruct((lines, 1), jnp.float32),
        ],
        compiler_params=pltpu.CompilerParams(vmem_limit_bytes=28 << 20),
        name="gradient_digits",
    )(place, near, far, values, other, earlier)


def hash_bytes(seeds, group, block):
    columns = lax.broadcasted_iota(jnp.int32, (seeds.shape[0], PROJECTED_BLOCK), 1)
    words = scramble((seeds + (group * PROJECTED_DIMS + block * PROJECTED_BLOCK)) + columns)
    found = []
    for byte in range(4):
        shifted = lax.shift_right_logical(words, jnp.full_like(words, 8 * byte)) if byte else words
        found.append(shifted.astype(jnp.int8))
    return found


def project_kernel(
    first_group, seeds_ref, digits_ref, scale_ref, before_ref, earlier_ref, out_ref, done_ref, total
):
    block, group = pl.program_id(0), pl.program_id(1)

    @pl.when(group == 0)
    def _():
        total[...] = jnp.zeros_like(total)
        done_ref[...] = scale_ref[...]

    found = hash_bytes(seeds_ref[...], first_group + group, block)
    signs = []
    for byte in range(4):
        for bit in range(8):
            is_set = (found[byte] & jnp.int8((1 << bit) - 256 * (bit == 7))) != 0
            signs.append(jnp.where(is_set, F8(-1), F8(1)))
    digits = jnp.concatenate([digits_ref[c] for c in range(32)], axis=1)
    total[...] += jnp.dot(
        digits, jnp.concatenate(signs, axis=0), preferred_element_type=jnp.float32
    )

    @pl.when(group == pl.num_programs(1) - 1)
    def _():
        examples = out_ref.shape[0]
        added = total[(DIGITS - 1) * examples :, :]
        for digit in reversed(range(DIGITS - 1)):
            added = added * (1 / DIGIT_STEP) + total[digit * examples : (digit + 1) * examples, :]
        out_ref[...] = before_ref[...] + added * scale_ref[...]


def project(seeds, digits, scale, before, first_group, skipped, groups, earlier):
    lines, rows = digits.shape[1:]
    examples = scale.shape[0]
    return pl.pallas_call(
        functools.partial(project_kernel, first_group + skipped),
        grid=(PROJECTED_DIMS // PROJECTED_BLOCK, groups),
        in_specs=[
            whole(seeds.shape),
            pl.BlockSpec((32, lines, rows), lambda k, g: (g + skipped, 0, 0)),
            whole((examples, 1)),
            pl.BlockSpec((examples, PROJECTED_BLOCK), lambda k, g: (0, k)),
            whole(earlier.shape),
        ],
        out_specs=[
            pl.BlockSpec((examples, PROJECTED_BLOCK), lambda k, g: (0, k)),
            whole((examples, 1)),
        ],
        out_shape=[
            jax.ShapeDtypeStruct((examples, PROJECTED_DIMS), jnp.float32),
            jax.ShapeDtypeStruct((examples, 1), jnp.float32),
        ],
        scratch_shapes=[pltpu.VMEM((lines, PROJECTED_BLOCK), jnp.float32)],
        cost_estimate=pl.CostEstimate(
            flops=2 * 256 * 32 * groups * rows * PROJECTED_DIMS, bytes_accessed=digits.size, transcendentals=0
        ),
        compiler_params=pltpu.CompilerParams(vmem_limit_bytes=32 << 20),
        name="project",
    )(seeds, digits, scale, before, earlier)


def shards(
    acts,
    output_gradients,
    adapter_down,
    adapter_up,
    lengths,
    sign_hash_seed,
    tile_indices,
    validation_projected,
    parts=2,
    chips=8,
):
    examples, width, tokens = acts.shape
    devices = 2 * chips
    half_examples = examples // 2
    group, chip, core = (lax.axis_index(name).astype(jnp.int32) for name in ("groups", "chip", "core"))
    place = jnp.stack([group, core])
    order = (jnp.arange(examples, dtype=jnp.int32) + (1 - core) * half_examples) % examples

    rank = adapter_down.shape[0]
    weights = (adapter_up, adapter_down)
    inputs = (output_gradients, acts)
    length = jnp.take(lengths, core * half_examples + chip * half_examples // chips).reshape(1)

    row_seeds = scramble(tile_indices + scramble(sign_hash_seed[0]))
    row_seeds = lax.dynamic_slice_in_dim(row_seeds, group * (width // 2), width // 2, 0)[:, None]

    def halves(values):
        sent = lax.dynamic_slice_in_dim(values, (1 - group) * (width // 2), width // 2, 1)
        return values, lax.ppermute(sent, "groups", [(0, 1), (1, 0)])

    def own_terms(half, earlier):
        sent, kept, done = partial_hidden(inputs[half], weights[half], lengths, order, half == 0, earlier)
        return kept + lax.ppermute(sent, "core", [(0, 1), (1, 0)]), done

    def exchange(terms):
        rows = terms.shape[0] * terms.shape[1] // chips
        return lax.all_to_all(terms.reshape(chips, rows, tokens), "chip", 0, 0, tiled=True)

    def spread(terms, earlier):
        copies, done = sum_terms(terms, length, parts * chips, earlier)
        near = lax.all_to_all(copies, ("groups", "chip"), 0, 0, tiled=True)
        return near.reshape(parts * half_examples, rank, tokens), done

    def digits_of(values, near, earlier):
        far = lax.ppermute(near, "core", [(0, 1), (1, 0)])
        return gradient_digits(near, far, *values, place, earlier)

    groups = rank // 32
    total = jnp.zeros((parts * examples, PROJECTED_DIMS), jnp.float32)
    terms, done = own_terms(0, order.reshape(1, examples))
    terms = exchange(terms)
    acts_halves = halves(acts)
    summed, done = spread(terms, done)
    terms, _ = own_terms(1, acts_halves[1][0, :8, :128])
    gradients_halves = halves(output_gradients)
    digits, scale = digits_of(acts_halves, summed, done)
    terms = exchange(after(terms, scale))
    total, done = project(row_seeds, digits, scale, total, 0, 0, 2, scale)
    summed, _ = spread(terms, done)
    total, done = project(row_seeds, digits, scale, total, 0, 2, groups - 2, scale)
    digits, scale = digits_of(gradients_halves, after(summed, done), done)
    projected, _ = project(row_seeds, digits, scale, total, groups, 0, groups, scale)

    local_k = validation_projected.shape[1]
    sent = projected.reshape(parts, examples, devices, local_k).transpose(0, 2, 1, 3)
    sent = sent.reshape(parts * devices, examples, local_k)
    own = lax.all_to_all(sent, ("groups", "chip", "core"), 0, 0, tiled=True).sum(0)

    inner = jnp.einsum("ek,vk->ev", own, validation_projected, precision=lax.Precision.HIGHEST)
    val_sq = jnp.sum(validation_projected * validation_projected, 1)
    train_sq = jnp.sum(own * own, 1)
    packed = jnp.concatenate(
        [inner, val_sq[None, :], jnp.pad(train_sq, (0, inner.shape[1] - examples))[None, :]], 0
    )
    packed = jnp.pad(packed, ((0, -packed.shape[0] % 8), (0, 0)))
    summed = lax.all_to_all(
        jnp.broadcast_to(packed[None], (devices,) + packed.shape), ("chip", "core"), 0, 0, tiled=True
    ).sum(0)
    train_norm = jnp.sqrt(summed[examples + 1, :examples] + 1e-06)
    val_norm = jnp.sqrt(summed[examples] + 1e-06)
    factor = math.sqrt(PROJECTED_DIMS)
    unit_grads = own * (factor / train_norm)[:, None]
    alignment = factor * summed[:examples] / (train_norm[:, None] * val_norm[None, :])
    task_score = jnp.mean(alignment.reshape(examples, TASKS, -1), 2)
    return (unit_grads, alignment, task_score)


def solution(mesh):
    groups, devices = mesh.shape["groups"], mesh.shape["mp"]
    chips = devices // 2
    mesh = Mesh(mesh.devices.reshape(groups, chips, 2), ("groups", "chip", "core"))
    split = ("chip", "core")
    placed = (
        P("groups", split, None),
        P("groups", split, None),
        P(None, split),
        P(split, None),
        P("groups"),
        P(),
        P(split),
        P("groups", split),
    )
    return jax.shard_map(
        functools.partial(shards, parts=groups, chips=chips),
        mesh=mesh,
        in_specs=placed,
        out_specs=(P("groups", split), P("groups", None), P("groups", None)),
        check_vma=False,
    )
```

time: 253 us -> 224 us (0.89)
  blocking collectives: 33.1 us -> 11.3 us
  waiting for transfers between devices: 51.1 us -> 33.8 us
  local copies, waits for them, and re-layouts: 6.21 us -> 14.9 us
  other arithmetic: 1.94 us -> 7.05 us
  Pallas kernels: 126 us -> 121 us
    all_to_all x6 -> x5, waiting for transfers between devices: 51.1 us -> 23.6 us  [the longest x2 11 us: exchange(): lax.all_to_all(terms.reshape(chips, rows, tokens), 'chip', 0, 0, tiled=True)]
    all_to_all x1 -> x0, blocking collectives: 21.9 us -> none  [shards(): lax.all_to_all(sent, 'mp', 0, 0, tiled=True).sum(0).astype(jnp.bfloat16)]
    ppermute x3 -> x6, waiting for transfers between devices: 0.01 us -> 10.2 us  [the longest x2 6.35 us: halves(): return (values, lax.ppermute(sent, 'groups', [(0, 1), (1, 0)]))]
    unnamed x20 -> x45, local copies, waits for them, and re-layouts: 2.65 us -> 9.26 us
    pallas_call x11, Pallas kernels: 126 us -> 121 us  [the longest x3 99.2 us: project(): pl.pallas_call(functools.partial(project_kernel, first_group + skipped),...]
    add x0 -> x2, other arithmetic: none -> 4.08 us  [own_terms(): return (kept + lax.ppermute(sent, 'core', [(0, 1), (1, 0)]), done)]
    dynamic_slice x0 -> x2, local copies, waits for them, and re-layouts: none -> 3.31 us  [halves(): lax.dynamic_slice_in_dim(values, (1 - group) * (width // 2), width // 2, 1)]
    all_to_all x6 -> x5, starting transfers between devices: 27.3 us -> 29 us  [the longest x2 12.4 us: exchange(): lax.all_to_all(terms.reshape(chips, rows, tokens), 'chip', 0, 0, tiled=True)]
  transfers between devices with their start and end apart: 9 -> 11, of which waited for: 5 -> 6; matrix products, arithmetic and copies ran while one was open for 1% -> 3% of each run, Pallas kernels for 26% -> 28%
where the time goes in v2:
time: 224 us; the launch traced here: 223 us
  Pallas kernels  121 us (54%)
  waiting for transfers between devices  33.8 us (15%)
  starting transfers between devices  32.2 us (14%)
  local copies, waits for them, and re-layouts  14.9 us (7%)
  blocking collectives  11.3 us (5%)
  other arithmetic  7.05 us (3%)
    pallas_call x3, Pallas kernels, project(): pl.pallas_call(functools.partial(project_kernel, first_group + skipped),...  99.2 us
    all_to_all x2, starting transfers between devices, exchange(): lax.all_to_all(terms.reshape(chips, rows, tokens), 'chip', 0, 0, tiled=True)  12.4 us
    all_to_all x1, blocking collectives, shards(): lax.all_to_all(jnp.broadcast_to(packed[None], (devices,) + packed.shape),...  11.3 us
    all_to_all x2, waiting for transfers between devices, exchange(): lax.all_to_all(terms.reshape(chips, rows, tokens), 'chip', 0, 0, tiled=True)  11 us
    all_to_all x2, starting transfers between devices, spread(): near = lax.all_to_all(copies, ('groups', 'chip'), 0, 0, tiled=True)  10.8 us
    all_to_all x1, waiting for transfers between devices, shards(): lax.all_to_all(sent, ('groups', 'chip', 'core'), 0, 0, tiled=True).sum(0)  10.2 us
    pallas_call x2, Pallas kernels, partial_hidden(): pl.pallas_call(functools.partial(hidden_kernel, masked, weight_dim), grid...  10.1 us
    unnamed x45, local copies, waits for them, and re-layouts  9.26 us
  transfers between devices with their start and end apart: 11, of which 6 were waited for; matrix products, arithmetic and copies ran while one was open for 3% of the time, Pallas kernels for 28%

profile of v2, /device:TPU:0, one launch (start us, length us, event | category | flops | bytes accessed | tf_op | source)
XLA Modules:
  0.0 222.9 jit_solution(5863276693521862192)
XLA Ops:
  0.6 0.6 and_select_fusion.1.order_ref
  1.2 0.5 and_select_fusion.earlier_ref
  1.7 5.1 %partial_hidden.3 = (f32[2,128,512]{2,1,0:T(8,128)}, f32[2,128,512]{2,1,0:T(8,128)}, s32[1,4]{1,0:T(1,128)}) custom-call(s32[4]{0:T(128)} %and_select_fusion.1.order_ref, s32[4]{0:T(128)} %lengths_ref.3, bf16[512,128]{1,0:T(8,128)(2,1)} %weight_ref.3, bf16[4,512,512]{2,1,0:T(8,128)(2,1)} %own_ref.3, s32[1,4]{1,0:T(1,128)} %and_select_fusion.earlier_ref), custom_call_target="tpu_custom_call" | custom-call | tf_op jit(solution)/shard_map/partial_hidden/pallas_call | solution.py:73
  6.8 0.5 collective-permute-start.2
  7.3 1.7 collective-permute-done.2
  9.0 1.9 add.94
  11.0 7.2 %all-to-all-start = ((f32[8,32,512]{2,1,0:T(8,128)}), f32[8,32,512]{2,1,0:T(8,128)S(1)}, u32[]{:S(2)}, u32[]{:S(2)}) async-start(f32[8,32,512]{2,1,0:T(8,128)} %bitcast.6), calls=%async_computation | async-start | bytes 1048576 | tf_op jit(solution)/shard_map/all_to_all | solution.py:283
  18.2 1.1 constant_dynamic-slice_fusion.1
  19.2 1.5 collective-permute-start
  20.7 0.6 dynamic-slice.2
  21.9 11.0 %all-to-all-done.terms_ref = f32[8,32,512]{2,1,0:T(8,128)S(1)} async-done(((f32[8,32,512]{2,1,0:T(8,128)}), f32[8,32,512]{2,1,0:T(8,128)S(1)}, u32[]{:S(2)}, u32[]{:S(2)}) %all-to-all-start) | async-done | bytes 524320 | tf_op jit(solution)/shard_map/all_to_all | solution.py:283
  32.9 0.8 copy-done.17
  33.7 1.9 sum_terms.2
  35.6 4.7 %all-to-all-start.1 = ((bf16[16,32,512]{2,1,0:T(8,128)(2,1)}), bf16[16,32,512]{2,1,0:T(8,128)(2,1)S(1)}, u32[]{:S(2)}, u32[]{:S(2)}) async-start(bf16[16,32,512]{2,1,0:T(8,128)(2,1)} %get-tuple-element.25), calls=%async_computation.1 | async-start | bytes 1048576 | tf_op jit(solution)/shard_map/all_to_all | solution.py:287
  40.3 6.3 %collective-permute-done.other_ref = bf16[4,256,512]{2,1,0:T(8,128)(2,1)S(1)} collective-permute-done((bf16[4,256,512]{2,1,0:T(8,128)(2,1)}, bf16[4,256,512]{2,1,0:T(8,128)(2,1)S(1)}, u32[]{:S(2)}, u32[]{:S(2)}) %collective-permute-start) | collective-permute-done | bytes 1048608 | tf_op jit(solution)/shard_map/ppermute | solution.py:275
  46.7 0.6 slice_bitcast_fusion.earlier_ref
  47.2 1.0 copy-done.5
  48.2 5.0 %partial_hidden.2 = (f32[2,128,512]{2,1,0:T(8,128)}, f32[2,128,512]{2,1,0:T(8,128)}, bf16[8,128]{1,0:T(8,128)(2,1)}) custom-call(s32[4]{0:T(128)} %and_select_fusion.1.order_ref, s32[4]{0:T(128)} %lengths_ref.3, bf16[128,512]{1,0:T(8,128)(2,1)} %weight_ref.2, bf16[4,512,512]{2,1,0:T(8,128)(2,1)} %own_ref.2, bf16[8,128]{1,0:T(8,128)(2,1)} %slice_bitcast_fusion.earlier_ref), custom_call_target="tpu_custom_call" | custom-call | tf_op jit(solution)/shard_map/partial_hidden/pallas_call | solution.py:73
  53.2 0.1 collective-permute-start.1
  53.3 2.4 %all-to-all-done.1 = bf16[16,32,512]{2,1,0:T(8,128)(2,1)S(1)} async-done(((bf16[16,32,512]{2,1,0:T(8,128)(2,1)}), bf16[16,32,512]{2,1,0:T(8,128)(2,1)S(1)}, u32[]{:S(2)}, u32[]{:S(2)}) %all-to-all-start.1) | async-done | bytes 524320 | tf_op jit(solution)/shard_map/all_to_all | solution.py:287
  55.7 0.0 collective-permute-start.3
  55.7 2.3 %constant_dynamic-slice_fusion = bf16[4,256,512]{2,1,0:T(8,128)(2,1)} fusion(bf16[4,512,512]{2,1,0:T(8,128)(2,1)} %own_ref.3, s32[]{:T(128)S(6)} %select_n.33), kind=kLoop, calls=%fused_computation.29 | loop fusion | bytes 2097156 | tf_op jit(solution)/shard_map/dynamic_slice | solution.py:274
  58.0 1.2 collective-permute-start.5
  59.9 0.1 dynamic_slice.9
  59.9 0.1 copy.24.seeds_ref
  60.1 0.1 pad_add_fusion.place_ref
  60.2 2.1 add.90.value_ref
  62.3 2.6 %gradient_digits.2 = (f8e4m3fn[128,32,256]{2,1,0:T(32,128)(4,1)S(1)}, f32[8,1]{1,0:T(8,128)S(1)}) custom-call(s32[2]{0:T(128)S(1)} %pad_add_fusion.place_ref, bf16[4,128,512]{2,1,0:T(8,128)(2,1)S(1)} %bitcast.30, bf16[4,128,512]{2,1,0:T(8,128)(2,1)S(1)} %collective-permute-done.3.far_ref, bf16[4,512,512]{2,1,0:T(8,128)(2,1)S(1)} %copy-done.1, ...), custom_call_target="tpu_custom_call" | custom-call | tf_op jit(solution)/shard_map/gradient_digits/pallas_call | solution.py:152
  64.9 0.0 copy-start.9
  64.9 0.6 copy-done.9
  65.5 1.0 copy-done.13
  66.5 0.8 after.2
  67.3 5.2 %all-to-all-start.2 = ((f32[8,32,512]{2,1,0:T(8,128)}), f32[8,32,512]{2,1,0:T(8,128)S(1)}, u32[]{:S(2)}, u32[]{:S(2)}) async-start(f32[8,32,512]{2,1,0:T(8,128)} %bitcast.32), calls=%async_computation.2 | async-start | bytes 1048576 | tf_op jit(solution)/shard_map/all_to_all | solution.py:283
  72.5 24.7 %project.3 = (f32[8,8192]{1,0:T(8,128)S(1)}, f32[8,1]{1,0:T(8,128)S(1)}) custom-call(s32[256,1]{1,0:T(8,128)S(1)} %copy.24.seeds_ref, f8e4m3fn[128,32,256]{2,1,0:T(32,128)(4,1)S(1)} %copy-done.14, f32[8,1]{1,0:T(8,128)S(1)} %copy-done.10, f32[8,8192]{1,0:T(8,128)S(1)} %broadcast_in_dim.31.before_ref, f32[8,1]{1,0:T(8,128)S(1)} %copy-done.10), custom_call_target="tpu_custom_call" | custom-call | flops 68719476736 | bytes 1048576 | tf_op jit(solution)/shard_map/project/pallas_call | solution.py:219
  97.2 0.0 copy-start.11
  97.2 0.6 copy-done.11
  97.8 0.8 copy-done.18
  98.6 1.9 sum_terms.3
  100.5 6.1 %all-to-all-start.3 = ((bf16[16,32,512]{2,1,0:T(8,128)(2,1)}), bf16[16,32,512]{2,1,0:T(8,128)(2,1)S(1)}, u32[]{:S(2)}, u32[]{:S(2)}) async-start(bf16[16,32,512]{2,1,0:T(8,128)(2,1)} %get-tuple-element.30), calls=%async_computation.3 | async-start | bytes 1048576 | tf_op jit(solution)/shard_map/all_to_all | solution.py:287
  106.6 1.2 copy-done.15
  107.8 24.7 %project.4 = (f32[8,8192]{1,0:T(8,128)S(1)}, f32[8,1]{1,0:T(8,128)S(1)}) custom-call(s32[256,1]{1,0:T(8,128)S(1)} %copy.24.seeds_ref, f8e4m3fn[128,32,256]{2,1,0:T(32,128)(4,1)S(1)} %copy-done.15, f32[8,1]{1,0:T(8,128)S(1)} %copy-done.10, f32[8,8192]{1,0:T(8,128)S(1)} %get-tuple-element.31.before_ref, f32[8,1]{1,0:T(8,128)S(1)} %copy-done.10), custom_call_target="tpu_custom_call" | custom-call | flops 68719476736 | bytes 1048576 | tf_op jit(solution)/shard_map/project/pallas_call | solution.py:219
  132.5 0.0 copy-start.7
  132.5 0.6 copy-done.7
  133.1 0.8 copy-done.3
  133.9 0.7 after.3.near_ref
  134.6 2.1 collective-permute-done.4.far_ref
  136.7 1.0 copy-done.4
  137.8 0.7 copy-done.8
  138.5 3.8 %gradient_digits.3 = (f8e4m3fn[128,32,256]{2,1,0:T(32,128)(4,1)S(1)}, f32[8,1]{1,0:T(8,128)S(1)}) custom-call(s32[2]{0:T(128)S(1)} %pad_add_fusion.place_ref, bf16[4,128,512]{2,1,0:T(8,128)(2,1)S(1)} %copy-done.4, bf16[4,128,512]{2,1,0:T(8,128)(2,1)S(1)} %collective-permute-done.4.far_ref, bf16[4,512,512]{2,1,0:T(8,128)(2,1)S(1)} %copy-done.2, ...), custom_call_target="tpu_custom_call" | custom-call | tf_op jit(solution)/shard_map/gradient_digits/pallas_call | solution.py:152
  142.3 49.8 %project.5 = (f32[8,8192]{1,0:T(8,128)S(1)}, f32[8,1]{1,0:T(8,128)}) custom-call(s32[256,1]{1,0:T(8,128)S(1)} %copy.24.seeds_ref, f8e4m3fn[128,32,256]{2,1,0:T(32,128)(4,1)S(1)} %get-tuple-element.33.digits_ref, f32[8,1]{1,0:T(8,128)S(1)} %get-tuple-element.34.scale_ref.earlier_ref, f32[8,8192]{1,0:T(8,128)S(1)} %get-tuple-element.35.before_ref, ...), custom_call_target="tpu_custom_call" | custom-call | flops 137438953472 | bytes 1048576 | tf_op jit(solution)/shard_map/project/pallas_call | solution.py:219
  192.0 0.2 copy.27
  192.2 0.9 copy.26
  193.1 5.9 %all-to-all-start.4 = ((f32[32,4,512]{2,1,0:T(4,128)}), f32[32,4,512]{2,1,0:T(4,128)S(1)}, u32[]{:S(2)}, u32[]{:S(2)}) async-start(f32[32,4,512]{2,1,0:T(4,128)} %copy.26), calls=%async_computation.4 | async-start | bytes 524288 | tf_op jit(solution)/shard_map/all_to_all | solution.py:313
  199.0 0.1 multiply_reduce_fusion
  199.1 10.2 %all-to-all-done.4 = f32[32,4,512]{2,1,0:T(4,128)S(1)} async-done(((f32[32,4,512]{2,1,0:T(4,128)}), f32[32,4,512]{2,1,0:T(4,128)S(1)}, u32[]{:S(2)}, u32[]{:S(2)}) %all-to-all-start.4) | async-done | bytes 262176 | tf_op jit(solution)/shard_map/all_to_all | solution.py:313
  209.3 0.1 reduce_sum.45
  209.3 0.5 fusion.6
  209.8 0.1 multiply_reduce_fusion.1
  210.0 11.3 %all_to_all.30 = f32[16,8,256]{2,1,0:T(8,128)S(1)} all-to-all(f32[16,8,256]{2,1,0:T(8,128)S(1)} %broadcast_in_dim.34), channel_id=1, replica_groups=mesh['groups'=2,'chip'=8,'core'=2] {'chip','core'}, dimensions={0} | all-to-all | bytes 262144 | tf_op jit(solution)/shard_map/all_to_all | solution.py:322
  221.4 0.1 fusion
  221.4 0.1 reshape.97
  221.5 0.1 reduce_sum.49
  221.6 0.6 broadcast_multiply_fusion.1
  222.2 0.7 broadcast_multiply_fusion
  (45 shorter events, 0.2 us)
Async XLA Ops:
  1.7 16.4 %copy-start = (bf16[4,512,512]{2,1,0:T(8,128)(2,1)S(1)}, bf16[4,512,512]{2,1,0:T(8,128)(2,1)}, u32[]{:S(2)}) copy-start(bf16[4,512,512]{2,1,0:T(8,128)(2,1)} %own_ref.2) | copy-start | bytes 6291460
  6.8 2.2 collective-permute-start.2
  9.0 11.7 %copy-start.20 = (s32[4]{0:T(128)S(1)}, s32[4]{0:T(128)}, u32[]{:S(2)}) copy-start(s32[4]{0:T(128)} %lengths_ref.3) | copy-start | bytes 52
  11.0 22.0 %all-to-all-start = ((f32[8,32,512]{2,1,0:T(8,128)}), f32[8,32,512]{2,1,0:T(8,128)S(1)}, u32[]{:S(2)}, u32[]{:S(2)}) async-start(f32[8,32,512]{2,1,0:T(8,128)} %bitcast.6), calls=%async_computation | async-start | bytes 1048576 | tf_op jit(solution)/shard_map/all_to_all | solution.py:283
  19.2 27.5 %collective-permute-start = (bf16[4,256,512]{2,1,0:T(8,128)(2,1)}, bf16[4,256,512]{2,1,0:T(8,128)(2,1)S(1)}, u32[]{:S(2)}, u32[]{:S(2)}) collective-permute-start(bf16[4,256,512]{2,1,0:T(8,128)(2,1)} %constant_dynamic-slice_fusion.1), channel_id=1, source_target_pairs={{0,16},{16,0},{1,17},{17,1},{2,18},{18,2},{3,19},{19,3},{4,20},{20... | collective-permute-start | bytes 3145736 | tf_op jit(solution)/shard_map/ppermute | solution.py:275
  32.9 0.8 copy-start.17
  35.6 20.1 %all-to-all-start.1 = ((bf16[16,32,512]{2,1,0:T(8,128)(2,1)}), bf16[16,32,512]{2,1,0:T(8,128)(2,1)S(1)}, u32[]{:S(2)}, u32[]{:S(2)}) async-start(bf16[16,32,512]{2,1,0:T(8,128)(2,1)} %get-tuple-element.25), calls=%async_computation.1 | async-start | bytes 1048576 | tf_op jit(solution)/shard_map/all_to_all | solution.py:287
  47.2 1.0 copy-start.5
  48.2 11.6 %copy-start.21 = (s32[512]{0:T(512)S(1)}, s32[512]{0:T(512)}, u32[]{:S(2)}) copy-start(s32[512]{0:T(512)} %param.14) | copy-start | bytes 6148
  53.2 9.1 %copy-start.1 = (bf16[4,512,512]{2,1,0:T(8,128)(2,1)S(1)}, bf16[4,512,512]{2,1,0:T(8,128)(2,1)}, u32[]{:S(2)}) copy-start(bf16[4,512,512]{2,1,0:T(8,128)(2,1)} %own_ref.2) | copy-start | bytes 6291460
  53.2 9.1 %copy-start.12 = (s32[1,4]{1,0:T(1,128)S(1)}, s32[1,4]{1,0:T(1,128)}, u32[]{:S(2)}) copy-start(s32[1,4]{1,0:T(1,128)} %get-tuple-element.26.earlier_ref) | copy-start | bytes 52
  53.2 6.9 %collective-permute-start.1 = (f32[2,128,512]{2,1,0:T(8,128)}, f32[2,128,512]{2,1,0:T(8,128)}, u32[]{:S(2)}, u32[]{:S(2)}) collective-permute-start(f32[2,128,512]{2,1,0:T(8,128)} %get-tuple-element.21), channel_id=1, source_target_pairs={{0,1},{1,0},{2,3},{3,2},{4,5},{5,4},{6,7},{7,6},{8,9},{9,8},{10,11... | collective-permute-start | bytes 1572872 | tf_op jit(solution)/shard_map/ppermute | solution.py:279
  55.7 6.6 %collective-permute-start.3 = (bf16[4,128,512]{2,1,0:T(8,128)(2,1)S(1)}, bf16[4,128,512]{2,1,0:T(8,128)(2,1)S(1)}, u32[]{:S(2)}, u32[]{:S(2)}) collective-permute-start(bf16[4,128,512]{2,1,0:T(8,128)(2,1)S(1)} %bitcast.29), channel_id=1, source_target_pairs={{0,1},{1,0},{2,3},{3,2},{4,5},{5,4},{6,7},{7,6},{8,9},{9,8},{10,11... | collective-permute-start | bytes 1572872 | tf_op jit(solution)/shard_map/ppermute | solution.py:291
  58.0 76.6 %collective-permute-start.5 = (bf16[4,256,512]{2,1,0:T(8,128)(2,1)}, bf16[4,256,512]{2,1,0:T(8,128)(2,1)}, u32[]{:S(2)}, u32[]{:S(2)}) collective-permute-start(bf16[4,256,512]{2,1,0:T(8,128)(2,1)} %constant_dynamic-slice_fusion), channel_id=1, source_target_pairs={{0,16},{16,0},{1,17},{17,1},{2,18},{18,2},{3,19},{19,3},{4,20},{20... | collective-permute-start | bytes 3145736 | tf_op jit(solution)/shard_map/ppermute | solution.py:275
  60.1 2.3 %copy-start.6 = (bf16[4,256,512]{2,1,0:T(8,128)(2,1)S(1)}, bf16[4,256,512]{2,1,0:T(8,128)(2,1)}, u32[]{:S(2)}) copy-start(bf16[4,256,512]{2,1,0:T(8,128)(2,1)} %copy-done.5) | copy-start | bytes 3145732
  64.9 0.6 copy-start.9
  65.5 1.0 copy-start.13
  66.5 6.0 %copy-start.10 = (f32[8,1]{1,0:T(8,128)S(1)}, f32[8,1]{1,0:T(8,128)}, u32[]{:S(2)}) copy-start(f32[8,1]{1,0:T(8,128)} %copy-done.9) | copy-start | bytes 100
  66.5 6.0 %copy-start.14 = (f8e4m3fn[128,32,256]{2,1,0:T(32,128)(4,1)S(1)}, f8e4m3fn[128,32,256]{2,1,0:T(32,128)(4,1)}, u32[]{:S(2)}) copy-start(f8e4m3fn[128,32,256]{2,1,0:T(32,128)(4,1)} %copy-done.13) | copy-start | bytes 3145732
  67.3 30.5 %all-to-all-start.2 = ((f32[8,32,512]{2,1,0:T(8,128)}), f32[8,32,512]{2,1,0:T(8,128)S(1)}, u32[]{:S(2)}, u32[]{:S(2)}) async-start(f32[8,32,512]{2,1,0:T(8,128)} %bitcast.32), calls=%async_computation.2 | async-start | bytes 1048576 | tf_op jit(solution)/shard_map/all_to_all | solution.py:283
  97.2 0.6 copy-start.11
  97.8 0.8 copy-start.18
  100.5 32.6 %all-to-all-start.3 = ((bf16[16,32,512]{2,1,0:T(8,128)(2,1)}), bf16[16,32,512]{2,1,0:T(8,128)(2,1)S(1)}, u32[]{:S(2)}, u32[]{:S(2)}) async-start(bf16[16,32,512]{2,1,0:T(8,128)(2,1)} %get-tuple-element.30), calls=%async_computation.3 | async-start | bytes 1048576 | tf_op jit(solution)/shard_map/all_to_all | solution.py:287
  106.6 1.2 copy-start.15
  107.8 28.9 %copy-start.2 = (bf16[4,512,512]{2,1,0:T(8,128)(2,1)S(1)}, bf16[4,512,512]{2,1,0:T(8,128)(2,1)}, u32[]{:S(2)}) copy-start(bf16[4,512,512]{2,1,0:T(8,128)(2,1)} %own_ref.3) | copy-start | bytes 6291460
  132.5 0.6 copy-start.7
  133.1 0.8 copy-start.3
  134.6 2.1 collective-permute-start.4
  136.7 1.0 copy-start.4
  137.8 0.7 copy-start.8
  192.0 6.9 %copy-start.16 = (f32[256,512]{1,0:T(8,128)S(1)}, f32[256,512]{1,0:T(8,128)}, u32[]{:S(2)}) copy-start(f32[256,512]{1,0:T(8,128)} %param.15) | copy-start | bytes 1572868
  193.1 16.2 %all-to-all-start.4 = ((f32[32,4,512]{2,1,0:T(4,128)}), f32[32,4,512]{2,1,0:T(4,128)S(1)}, u32[]{:S(2)}, u32[]{:S(2)}) async-start(f32[32,4,512]{2,1,0:T(4,128)} %copy.26), calls=%async_computation.4 | async-start | bytes 524288 | tf_op jit(solution)/shard_map/all_to_all | solution.py:313
  221.4 1.4 copy-start.19

commit v3 on v2

--- a/solution.py
+++ b/solution.py
@@ -34,24 +34,52 @@
 def after(value, earlier):
     return pl.pallas_call(
         lambda value_ref, earlier_ref, out_ref: None,
+        grid=(1,),
         in_specs=[pl.BlockSpec(memory_space=pl.ANY), whole(earlier.shape)],
         out_specs=pl.BlockSpec(memory_space=pl.ANY),
         out_shape=jax.ShapeDtypeStruct(value.shape, value.dtype),
         input_output_aliases={0: 0},
-        grid=(1,),
         name="after",
     )(value, earlier)
 
 
-def hidden_kernel(masked, weight_dim, order_ref, lengths_ref, weight_ref, values_ref, earlier_ref, sent_ref, kept_ref, done_ref):
+def add_kernel(kept_ref, received_ref, earlier_ref, out_ref):
+    out_ref[...] = kept_ref[...] + received_ref[...]
+
+
+def add_terms(kept, received, earlier):
+    return pl.pallas_call(
+        add_kernel,
+        grid=(kept.shape[0],),
+        in_specs=[pl.BlockSpec((1,) + kept.shape[1:], lambda e: (e, 0, 0))] * 2 + [whole(earlier.shape)],
+        out_specs=pl.BlockSpec((1,) + kept.shape[1:], lambda e: (e, 0, 0)),
+        out_shape=jax.ShapeDtypeStruct(kept.shape, kept.dtype),
+        name="add_terms",
+    )(kept, received, earlier)
+
+
+def sender_order(step, place, examples):
+    return lax.rem(step + (1 - place[1]) * (examples // 2), examples)
+
+
+def hidden_kernel(masked, follows, place_ref, lengths_ref, weight_ref, values_ref, *rest):
     step = pl.program_id(0)
+    if follows:
+        earlier_ref, passed_ref, copied_ref, sent_ref, kept_ref, done_ref = rest
+        copied_ref[...] = passed_ref[...]
+    else:
+        sent_ref, kept_ref, done_ref = rest
     product = lax.dot_general(
-        weight_ref[...], values_ref[0], (((weight_dim,), (0,)), ((), ())), preferred_element_type=jnp.float32
+        weight_ref[...],
+        values_ref[0],
+        (((0 if masked else 1,), (0,)), ((), ())),
+        preferred_element_type=jnp.float32,
     )
     if masked:
         positions = lax.broadcasted_iota(jnp.int32, product.shape, 1)
-        product = jnp.where(positions < lengths_ref[order_ref[step]], product, 0.0)
-    early = step < sent_ref.shape[0] * (pl.num_programs(0) // 2)
+        example = sender_order(step, place_ref, pl.num_programs(0))
+        product = jnp.where(positions < lengths_ref[example], product, 0.0)
+    early = step < pl.num_programs(0) // 2
 
     @pl.when(early)
     def _():
@@ -61,35 +89,44 @@
     def _():
         kept_ref[0] = product
 
-    done_ref[...] = earlier_ref[...]
-
-
-def partial_hidden(values, weight, lengths, order, masked, earlier):
+    done_ref[...] = jnp.zeros_like(done_ref)
+
+
+def partial_hidden(values, weight, lengths, place, masked, earlier=None, passed=None):
     examples, width, tokens = values.shape
-    weight_dim = 0 if masked else 1
-    count = weight.shape[1 - weight_dim]
+    count = weight.shape[1 if masked else 0]
     half = examples // 2
+    rows = width // 2
+    follows = earlier is not None
+    in_specs = [
+        pl.BlockSpec(memory_space=pltpu.SMEM),
+        whole(weight.shape),
+        pl.BlockSpec((1, width, tokens), lambda e, place: (sender_order(e, place, examples), 0, 0)),
+    ]
+    out_specs = [
+        pl.BlockSpec((1, count, tokens), lambda e, place: (jnp.minimum(e, half - 1), 0, 0)),
+        pl.BlockSpec((1, count, tokens), lambda e, place: (jnp.maximum(e - half, 0), 0, 0)),
+        whole((8, 1)),
+    ]
     shape = jax.ShapeDtypeStruct((half, count, tokens), jnp.float32)
-    return pl.pallas_call(
-        functools.partial(hidden_kernel, masked, weight_dim),
+    out_shape = [shape, shape, jax.ShapeDtypeStruct((8, 1), jnp.float32)]
+    operands = [place, lengths, weight, values]
+    if follows:
+        in_specs += [
+            whole(earlier.shape),
+            pl.BlockSpec((1, rows, tokens), lambda e, place: (e, 1 - place[0], 0)),
+        ]
+        out_specs = [pl.BlockSpec((1, rows, tokens), lambda e, place: (e, 0, 0))] + out_specs
+        out_shape = [jax.ShapeDtypeStruct((examples, rows, tokens), passed.dtype)] + out_shape
+        operands += [earlier, passed]
+    return pl.pallas_call(
+        functools.partial(hidden_kernel, masked, follows),
         grid_spec=pltpu.PrefetchScalarGridSpec(
-            num_scalar_prefetch=1,
-            grid=(examples,),
-            in_specs=[
-                pl.BlockSpec(memory_space=pltpu.SMEM),
-                whole(weight.shape),
-                pl.BlockSpec((1, width, tokens), lambda e, order: (order[e], 0, 0)),
-                whole(earlier.shape),
-            ],
-            out_specs=[
-                pl.BlockSpec((1, count, tokens), lambda e, order: (jnp.minimum(e, half - 1), 0, 0)),
-                pl.BlockSpec((1, count, tokens), lambda e, order: (jnp.maximum(e - half, 0), 0, 0)),
-                whole(earlier.shape),
-            ],
+            num_scalar_prefetch=1, grid=(examples,), in_specs=in_specs, out_specs=out_specs
         ),
-        out_shape=[shape, shape, jax.ShapeDtypeStruct(earlier.shape, earlier.dtype)],
+        out_shape=out_shape,
         name="partial_hidden",
-    )(order, lengths, weight, values, earlier)
+    )(*operands)
 
 
 def sum_kernel(length_ref, terms_ref, earlier_ref, out_ref, done_ref):
@@ -260,23 +297,14 @@
     half_examples = examples // 2
     group, chip, core = (lax.axis_index(name).astype(jnp.int32) for name in ("groups", "chip", "core"))
     place = jnp.stack([group, core])
-    order = (jnp.arange(examples, dtype=jnp.int32) + (1 - core) * half_examples) % examples
-
     rank = adapter_down.shape[0]
-    weights = (adapter_up, adapter_down)
-    inputs = (output_gradients, acts)
     length = jnp.take(lengths, core * half_examples + chip * half_examples // chips).reshape(1)
 
     row_seeds = scramble(tile_indices + scramble(sign_hash_seed[0]))
     row_seeds = lax.dynamic_slice_in_dim(row_seeds, group * (width // 2), width // 2, 0)[:, None]
 
-    def halves(values):
-        sent = lax.dynamic_slice_in_dim(values, (1 - group) * (width // 2), width // 2, 1)
-        return values, lax.ppermute(sent, "groups", [(0, 1), (1, 0)])
-
-    def own_terms(half, earlier):
-        sent, kept, done = partial_hidden(inputs[half], weights[half], lengths, order, half == 0, earlier)
-        return kept + lax.ppermute(sent, "core", [(0, 1), (1, 0)]), done
+    def swap(values, name):
+        return lax.ppermute(values, name, [(0, 1), (1, 0)])
 
     def exchange(terms):
         rows = terms.shape[0] * terms.shape[1] // chips
@@ -288,23 +316,27 @@
         return near.reshape(parts * half_examples, rank, tokens), done
 
     def digits_of(values, near, earlier):
-        far = lax.ppermute(near, "core", [(0, 1), (1, 0)])
+        far = swap(near, "core")
         return gradient_digits(near, far, *values, place, earlier)
 
     groups = rank // 32
     total = jnp.zeros((parts * examples, PROJECTED_DIMS), jnp.float32)
-    terms, done = own_terms(0, order.reshape(1, examples))
-    terms = exchange(terms)
-    acts_halves = halves(acts)
+    sent, kept, done = partial_hidden(output_gradients, adapter_up, lengths, place, True)
+    terms = exchange(kept + swap(sent, "core"))
+    acts_sent = lax.dynamic_slice_in_dim(acts, (1 - group) * (width // 2), width // 2, 1)
+    acts_other = swap(acts_sent, "groups")
     summed, done = spread(terms, done)
-    terms, _ = own_terms(1, acts_halves[1][0, :8, :128])
-    gradients_halves = halves(output_gradients)
-    digits, scale = digits_of(acts_halves, summed, done)
-    terms = exchange(after(terms, scale))
+    gradients_sent, sent, kept, _ = partial_hidden(
+        acts, adapter_down, lengths, place, False, acts_other[0, :8, :128], output_gradients
+    )
+    gradients_other = swap(gradients_sent, "groups")
+    received = swap(sent, "core")
+    digits, scale = digits_of((acts, acts_other), summed, received[0, :8, :128])
+    terms = exchange(add_terms(kept, received, scale))
     total, done = project(row_seeds, digits, scale, total, 0, 0, 2, scale)
     summed, _ = spread(terms, done)
     total, done = project(row_seeds, digits, scale, total, 0, 2, groups - 2, scale)
-    digits, scale = digits_of(gradients_halves, after(summed, done), done)
+    digits, scale = digits_of((output_gradients, gradients_other), after(summed, done), done)
     projected, _ = project(row_seeds, digits, scale, total, groups, 0, groups, scale)
 
     local_k = validation_projected.shape[1]

time: 224 us -> 223 us (level)
  other arithmetic: 7.05 us -> 4.32 us
    dynamic_slice x2 -> x1, local copies, waits for them, and re-layouts: 3.31 us -> 1.05 us  [shards(): lax.dynamic_slice_in_dim(acts, (1 - group) * (width // 2), width // 2, 1)]
  transfers between devices with their start and end apart: 11 -> 11, of which waited for: 6 -> 6; matrix products, arithmetic and copies ran while one was open for 3% -> 1% of each run, Pallas kernels for 28% -> 29%
where the time goes in v3:
time: 223 us; the launch traced here: 222 us
  Pallas kernels  123 us (55%)
  waiting for transfers between devices  33.4 us (15%)
  starting transfers between devices  32.7 us (15%)
  local copies, waits for them, and re-layouts  14.6 us (7%)
  blocking collectives  11.3 us (5%)
  other arithmetic  4.32 us (2%)
    pallas_call x3, Pallas kernels, project(): pl.pallas_call(functools.partial(project_kernel, first_group + skipped),...  99.2 us
    all_to_all x2, starting transfers between devices, exchange(): lax.all_to_all(terms.reshape(chips, rows, tokens), 'chip', 0, 0, tiled=True)  12.7 us
    all_to_all x1, blocking collectives, shards(): lax.all_to_all(jnp.broadcast_to(packed[None], (devices,) + packed.shape),...  11.3 us
    all_to_all x2, waiting for transfers between devices, exchange(): lax.all_to_all(terms.reshape(chips, rows, tokens), 'chip', 0, 0, tiled=True)  11 us
    all_to_all x2, starting transfers between devices, spread(): near = lax.all_to_all(copies, ('groups', 'chip'), 0, 0, tiled=True)  11 us
    pallas_call x2, Pallas kernels, partial_hidden(): pl.pallas_call(functools.partial(hidden_kernel, masked, follows), grid_sp...  10.5 us
    unnamed x45, local copies, waits for them, and re-layouts  10.5 us
    ppermute x6, waiting for transfers between devices, swap(): return lax.ppermute(values, name, [(0, 1), (1, 0)])  10.2 us
  transfers between devices with their start and end apart: 11, of which 6 were waited for; matrix products, arithmetic and copies ran while one was open for 1% of the time, Pallas kernels for 29%

profile of v3, /device:TPU:0, one launch (start us, length us, event | category | flops | bytes accessed | tf_op | source)
XLA Modules:
  0.0 221.6 jit_solution(7382147643642400547)
XLA Ops:
  0.6 0.6 pad_add_fusion.place_ref
  1.2 5.1 %partial_hidden.3 = (f32[2,128,512]{2,1,0:T(8,128)}, f32[2,128,512]{2,1,0:T(8,128)}, f32[8,1]{1,0:T(8,128)}) custom-call(s32[2]{0:T(128)} %pad_add_fusion.place_ref, s32[4]{0:T(128)} %lengths_ref.3, bf16[512,128]{1,0:T(8,128)(2,1)} %weight_ref.3, bf16[4,512,512]{2,1,0:T(8,128)(2,1)} %own_ref.3), custom_call_target="tpu_custom_call" | custom-call | tf_op jit(solution)/shard_map/partial_hidden/pallas_call | solution.py:122
  6.3 0.5 collective-permute-start.2
  6.8 1.7 collective-permute-done.2
  8.5 1.9 add.51
  10.4 7.2 %all-to-all-start = ((f32[8,32,512]{2,1,0:T(8,128)}), f32[8,32,512]{2,1,0:T(8,128)S(1)}, u32[]{:S(2)}, u32[]{:S(2)}) async-start(f32[8,32,512]{2,1,0:T(8,128)} %bitcast.6), calls=%async_computation | async-start | bytes 1048576 | tf_op jit(solution)/shard_map/all_to_all | solution.py:311
  17.6 1.0 constant_dynamic-slice_fusion
  18.7 1.5 collective-permute-start
  20.2 0.6 dynamic-slice.2
  21.4 11.0 %all-to-all-done.terms_ref = f32[8,32,512]{2,1,0:T(8,128)S(1)} async-done(((f32[8,32,512]{2,1,0:T(8,128)}), f32[8,32,512]{2,1,0:T(8,128)S(1)}, u32[]{:S(2)}, u32[]{:S(2)}) %all-to-all-start) | async-done | bytes 524320 | tf_op jit(solution)/shard_map/all_to_all | solution.py:311
  32.4 0.8 copy-done.17
  33.2 1.9 sum_terms.2
  35.1 4.7 %all-to-all-start.1 = ((bf16[16,32,512]{2,1,0:T(8,128)(2,1)}), bf16[16,32,512]{2,1,0:T(8,128)(2,1)S(1)}, u32[]{:S(2)}, u32[]{:S(2)}) async-start(bf16[16,32,512]{2,1,0:T(8,128)(2,1)} %get-tuple-element.25), calls=%async_computation.1 | async-start | bytes 1048576 | tf_op jit(solution)/shard_map/all_to_all | solution.py:315
  39.8 6.4 %collective-permute-done.other_ref = bf16[4,256,512]{2,1,0:T(8,128)(2,1)S(1)} collective-permute-done((bf16[4,256,512]{2,1,0:T(8,128)(2,1)}, bf16[4,256,512]{2,1,0:T(8,128)(2,1)S(1)}, u32[]{:S(2)}, u32[]{:S(2)}) %collective-permute-start) | collective-permute-done | bytes 1048608 | tf_op jit(solution)/shard_map/ppermute | solution.py:307
  46.2 0.6 slice_bitcast_fusion.1.rest_0_
  46.7 1.0 copy-done.5
  47.7 5.4 %partial_hidden.2 = (bf16[4,256,512]{2,1,0:T(8,128)(2,1)}, f32[2,128,512]{2,1,0:T(8,128)}, f32[2,128,512]{2,1,0:T(8,128)}, f32[8,1]{1,0:T(8,128)}) custom-call(s32[2]{0:T(128)} %pad_add_fusion.place_ref, s32[4]{0:T(128)} %lengths_ref.3, bf16[128,512]{1,0:T(8,128)(2,1)} %weight_ref.2, bf16[4,512,512]{2,1,0:T(8,128)(2,1)} %own_ref.2, ...), custom_call_target="tpu_custom_call" | custom-call | tf_op jit(solution)/shard_map/partial_hidden/pallas_call | solution.py:122
  53.1 0.0 collective-permute-start.1
  53.1 2.1 all-to-all-done.1
  55.9 0.1 dynamic_slice.6
  56.0 0.1 copy.23.seeds_ref
  56.1 1.3 collective-permute-start.5
  57.4 0.0 collective-permute-done.1.received_ref
  57.4 0.7 slice_bitcast_fusion.earlier_ref
  58.1 1.2 copy-done.6
  59.3 2.6 %gradient_digits.2 = (f8e4m3fn[128,32,256]{2,1,0:T(32,128)(4,1)S(1)}, f32[8,1]{1,0:T(8,128)S(1)}) custom-call(s32[2]{0:T(128)S(1)} %copy-done.9, bf16[4,128,512]{2,1,0:T(8,128)(2,1)S(1)} %bitcast.32, bf16[4,128,512]{2,1,0:T(8,128)(2,1)S(1)} %collective-permute-done.3.far_ref, bf16[4,512,512]{2,1,0:T(8,128)(2,1)S(1)} %copy-done.2, ...), custom_call_target="tpu_custom_call" | custom-call | tf_op jit(solution)/shard_map/gradient_digits/pallas_call | solution.py:189
  61.8 0.0 copy-start.10
  61.9 0.6 copy-done.10
  62.4 1.0 copy-done.13
  63.4 2.0 add_terms.1
  65.5 5.5 %all-to-all-start.2 = ((f32[8,32,512]{2,1,0:T(8,128)}), f32[8,32,512]{2,1,0:T(8,128)S(1)}, u32[]{:S(2)}, u32[]{:S(2)}) async-start(f32[8,32,512]{2,1,0:T(8,128)} %bitcast.34), calls=%async_computation.2 | async-start | bytes 1048576 | tf_op jit(solution)/shard_map/all_to_all | solution.py:311
  71.0 24.7 %project.3 = (f32[8,8192]{1,0:T(8,128)S(1)}, f32[8,1]{1,0:T(8,128)S(1)}) custom-call(s32[256,1]{1,0:T(8,128)S(1)} %copy.23.seeds_ref, f8e4m3fn[128,32,256]{2,1,0:T(32,128)(4,1)S(1)} %copy-done.14, f32[8,1]{1,0:T(8,128)S(1)} %copy-done.11, f32[8,8192]{1,0:T(8,128)S(1)} %broadcast_in_dim.31.before_ref, f32[8,1]{1,0:T(8,128)S(1)} %copy-done.11), custom_call_target="tpu_custom_call" | custom-call | flops 68719476736 | bytes 1048576 | tf_op jit(solution)/shard_map/project/pallas_call | solution.py:256
  95.7 0.0 copy-start.12
  95.7 0.6 copy-done.12
  96.3 0.0 all-to-all-done.2.terms_ref
  96.3 0.8 copy-done.18
  97.1 1.9 sum_terms.3
  99.0 6.3 %all-to-all-start.3 = ((bf16[16,32,512]{2,1,0:T(8,128)(2,1)}), bf16[16,32,512]{2,1,0:T(8,128)(2,1)S(1)}, u32[]{:S(2)}, u32[]{:S(2)}) async-start(bf16[16,32,512]{2,1,0:T(8,128)(2,1)} %get-tuple-element.29), calls=%async_computation.3 | async-start | bytes 1048576 | tf_op jit(solution)/shard_map/all_to_all | solution.py:315
  105.3 1.2 copy-done.15
  106.5 24.7 %project.4 = (f32[8,8192]{1,0:T(8,128)S(1)}, f32[8,1]{1,0:T(8,128)S(1)}) custom-call(s32[256,1]{1,0:T(8,128)S(1)} %copy.23.seeds_ref, f8e4m3fn[128,32,256]{2,1,0:T(32,128)(4,1)S(1)} %copy-done.15, f32[8,1]{1,0:T(8,128)S(1)} %copy-done.11, f32[8,8192]{1,0:T(8,128)S(1)} %get-tuple-element.30.before_ref, f32[8,1]{1,0:T(8,128)S(1)} %copy-done.11), custom_call_target="tpu_custom_call" | custom-call | flops 68719476736 | bytes 1048576 | tf_op jit(solution)/shard_map/project/pallas_call | solution.py:256
  131.2 0.0 copy-start.7
  131.2 0.6 copy-done.7
  131.8 0.0 all-to-all-done.3
  131.8 0.8 copy-done.3
  132.6 0.7 after.1.near_ref
  133.3 2.1 collective-permute-done.4.far_ref
  135.4 1.0 copy-done.4
  136.5 0.7 copy-done.8
  137.2 3.8 %gradient_digits.3 = (f8e4m3fn[128,32,256]{2,1,0:T(32,128)(4,1)S(1)}, f32[8,1]{1,0:T(8,128)S(1)}) custom-call(s32[2]{0:T(128)S(1)} %copy-done.9, bf16[4,128,512]{2,1,0:T(8,128)(2,1)S(1)} %copy-done.4, bf16[4,128,512]{2,1,0:T(8,128)(2,1)S(1)} %collective-permute-done.4.far_ref, bf16[4,512,512]{2,1,0:T(8,128)(2,1)S(1)} %copy-done, ...), custom_call_target="tpu_custom_call" | custom-call | tf_op jit(solution)/shard_map/gradient_digits/pallas_call | solution.py:189
  141.0 49.8 %project.5 = (f32[8,8192]{1,0:T(8,128)S(1)}, f32[8,1]{1,0:T(8,128)}) custom-call(s32[256,1]{1,0:T(8,128)S(1)} %copy.23.seeds_ref, f8e4m3fn[128,32,256]{2,1,0:T(32,128)(4,1)S(1)} %get-tuple-element.33.digits_ref, f32[8,1]{1,0:T(8,128)S(1)} %get-tuple-element.34.scale_ref.earlier_ref, f32[8,8192]{1,0:T(8,128)S(1)} %get-tuple-element.35.before_ref, ...), custom_call_target="tpu_custom_call" | custom-call | flops 137438953472 | bytes 1048576 | tf_op jit(solution)/shard_map/project/pallas_call | solution.py:256
  190.7 0.2 copy.26
  190.9 0.9 copy.25
  191.8 5.9 %all-to-all-start.4 = ((f32[32,4,512]{2,1,0:T(4,128)}), f32[32,4,512]{2,1,0:T(4,128)S(1)}, u32[]{:S(2)}, u32[]{:S(2)}) async-start(f32[32,4,512]{2,1,0:T(4,128)} %copy.25), calls=%async_computation.4 | async-start | bytes 524288 | tf_op jit(solution)/shard_map/all_to_all | solution.py:345
  197.7 0.1 multiply_reduce_fusion
  197.8 10.2 %all-to-all-done.4 = f32[32,4,512]{2,1,0:T(4,128)S(1)} async-done(((f32[32,4,512]{2,1,0:T(4,128)}), f32[32,4,512]{2,1,0:T(4,128)S(1)}, u32[]{:S(2)}, u32[]{:S(2)}) %all-to-all-start.4) | async-done | bytes 262176 | tf_op jit(solution)/shard_map/all_to_all | solution.py:345
  208.0 0.1 reduce_sum.45
  208.0 0.5 fusion.4
  208.5 0.1 multiply_reduce_fusion.1
  208.7 11.3 %all_to_all.30 = f32[16,8,256]{2,1,0:T(8,128)S(1)} all-to-all(f32[16,8,256]{2,1,0:T(8,128)S(1)} %broadcast_in_dim.34), channel_id=1, replica_groups=mesh['groups'=2,'chip'=8,'core'=2] {'chip','core'}, dimensions={0} | all-to-all | bytes 262144 | tf_op jit(solution)/shard_map/all_to_all | solution.py:354
  220.0 0.1 fusion
  220.1 0.1 reshape.56
  220.2 0.1 reduce_sum.49
  220.3 0.6 broadcast_multiply_fusion.1
  220.9 0.7 broadcast_multiply_fusion
  (42 shorter events, 0.2 us)
Async XLA Ops:
  1.2 16.4 %copy-start.1 = (bf16[4,512,512]{2,1,0:T(8,128)(2,1)S(1)}, bf16[4,512,512]{2,1,0:T(8,128)(2,1)}, u32[]{:S(2)}) copy-start(bf16[4,512,512]{2,1,0:T(8,128)(2,1)} %own_ref.2) | copy-start | bytes 6291460
  6.3 2.2 collective-permute-start.2
  8.5 11.7 %copy-start.21 = (s32[4]{0:T(128)S(1)}, s32[4]{0:T(128)}, u32[]{:S(2)}) copy-start(s32[4]{0:T(128)} %lengths_ref.3) | copy-start | bytes 52
  10.4 22.0 %all-to-all-start = ((f32[8,32,512]{2,1,0:T(8,128)}), f32[8,32,512]{2,1,0:T(8,128)S(1)}, u32[]{:S(2)}, u32[]{:S(2)}) async-start(f32[8,32,512]{2,1,0:T(8,128)} %bitcast.6), calls=%async_computation | async-start | bytes 1048576 | tf_op jit(solution)/shard_map/all_to_all | solution.py:311
  18.7 27.5 %collective-permute-start = (bf16[4,256,512]{2,1,0:T(8,128)(2,1)}, bf16[4,256,512]{2,1,0:T(8,128)(2,1)S(1)}, u32[]{:S(2)}, u32[]{:S(2)}) collective-permute-start(bf16[4,256,512]{2,1,0:T(8,128)(2,1)} %constant_dynamic-slice_fusion), channel_id=1, source_target_pairs={{0,16},{16,0},{1,17},{17,1},{2,18},{18,2},{3,19},{19,3},{4,20},{20... | collective-permute-start | bytes 3145736 | tf_op jit(solution)/shard_map/ppermute | solution.py:307
  32.4 0.8 copy-start.17
  35.1 20.1 %all-to-all-start.1 = ((bf16[16,32,512]{2,1,0:T(8,128)(2,1)}), bf16[16,32,512]{2,1,0:T(8,128)(2,1)S(1)}, u32[]{:S(2)}, u32[]{:S(2)}) async-start(bf16[16,32,512]{2,1,0:T(8,128)(2,1)} %get-tuple-element.25), calls=%async_computation.1 | async-start | bytes 1048576 | tf_op jit(solution)/shard_map/all_to_all | solution.py:315
  46.7 1.0 copy-start.5
  47.7 8.1 %copy-start.20 = (s32[512]{0:T(512)S(1)}, s32[512]{0:T(512)}, u32[]{:S(2)}) copy-start(s32[512]{0:T(512)} %param.14) | copy-start | bytes 6148
  47.7 10.3 %copy-start.2 = (bf16[4,512,512]{2,1,0:T(8,128)(2,1)S(1)}, bf16[4,512,512]{2,1,0:T(8,128)(2,1)}, u32[]{:S(2)}) copy-start(bf16[4,512,512]{2,1,0:T(8,128)(2,1)} %own_ref.2) | copy-start | bytes 6291460
  47.7 10.3 %copy-start.9 = (s32[2]{0:T(128)S(1)}, s32[2]{0:T(128)}, u32[]{:S(2)}) copy-start(s32[2]{0:T(128)} %pad_add_fusion.place_ref) | copy-start | bytes 28
  53.1 4.3 %collective-permute-start.1 = (f32[2,128,512]{2,1,0:T(8,128)}, f32[2,128,512]{2,1,0:T(8,128)}, u32[]{:S(2)}, u32[]{:S(2)}) collective-permute-start(f32[2,128,512]{2,1,0:T(8,128)} %get-tuple-element.21), channel_id=1, source_target_pairs={{0,1},{1,0},{2,3},{3,2},{4,5},{5,4},{6,7},{7,6},{8,9},{9,8},{10,11... | collective-permute-start | bytes 1572872 | tf_op jit(solution)/shard_map/ppermute | solution.py:307
  55.2 2.9 %collective-permute-start.3 = (bf16[4,128,512]{2,1,0:T(8,128)(2,1)S(1)}, bf16[4,128,512]{2,1,0:T(8,128)(2,1)S(1)}, u32[]{:S(2)}, u32[]{:S(2)}) collective-permute-start(bf16[4,128,512]{2,1,0:T(8,128)(2,1)S(1)} %bitcast.31), channel_id=1, source_target_pairs={{0,1},{1,0},{2,3},{3,2},{4,5},{5,4},{6,7},{7,6},{8,9},{9,8},{10,11... | collective-permute-start | bytes 1572872 | tf_op jit(solution)/shard_map/ppermute | solution.py:307
  56.1 77.2 %collective-permute-start.5 = (bf16[4,256,512]{2,1,0:T(8,128)(2,1)}, bf16[4,256,512]{2,1,0:T(8,128)(2,1)}, u32[]{:S(2)}, u32[]{:S(2)}) collective-permute-start(bf16[4,256,512]{2,1,0:T(8,128)(2,1)} %get-tuple-element.32), channel_id=1, source_target_pairs={{0,16},{16,0},{1,17},{17,1},{2,18},{18,2},{3,19},{19,3},{4,20},{20... | collective-permute-start | bytes 3145736 | tf_op jit(solution)/shard_map/ppermute | solution.py:307
  58.1 1.2 copy-start.6
  61.8 0.6 copy-start.10
  62.4 1.0 copy-start.13
  63.4 7.5 %copy-start.11 = (f32[8,1]{1,0:T(8,128)S(1)}, f32[8,1]{1,0:T(8,128)}, u32[]{:S(2)}) copy-start(f32[8,1]{1,0:T(8,128)} %copy-done.10) | copy-start | bytes 100
  63.4 7.5 %copy-start.14 = (f8e4m3fn[128,32,256]{2,1,0:T(32,128)(4,1)S(1)}, f8e4m3fn[128,32,256]{2,1,0:T(32,128)(4,1)}, u32[]{:S(2)}) copy-start(f8e4m3fn[128,32,256]{2,1,0:T(32,128)(4,1)} %copy-done.13) | copy-start | bytes 3145732
  65.5 30.8 %all-to-all-start.2 = ((f32[8,32,512]{2,1,0:T(8,128)}), f32[8,32,512]{2,1,0:T(8,128)S(1)}, u32[]{:S(2)}, u32[]{:S(2)}) async-start(f32[8,32,512]{2,1,0:T(8,128)} %bitcast.34), calls=%async_computation.2 | async-start | bytes 1048576 | tf_op jit(solution)/shard_map/all_to_all | solution.py:311
  95.7 0.6 copy-start.12
  96.3 0.8 copy-start.18
  99.0 32.8 %all-to-all-start.3 = ((bf16[16,32,512]{2,1,0:T(8,128)(2,1)}), bf16[16,32,512]{2,1,0:T(8,128)(2,1)S(1)}, u32[]{:S(2)}, u32[]{:S(2)}) async-start(bf16[16,32,512]{2,1,0:T(8,128)(2,1)} %get-tuple-element.29), calls=%async_computation.3 | async-start | bytes 1048576 | tf_op jit(solution)/shard_map/all_to_all | solution.py:315
  105.3 1.2 copy-start.15
  106.5 28.9 %copy-start = (bf16[4,512,512]{2,1,0:T(8,128)(2,1)S(1)}, bf16[4,512,512]{2,1,0:T(8,128)(2,1)}, u32[]{:S(2)}) copy-start(bf16[4,512,512]{2,1,0:T(8,128)(2,1)} %own_ref.3) | copy-start | bytes 6291460
  131.2 0.6 copy-start.7
  131.8 0.8 copy-start.3
  133.3 2.1 collective-permute-start.4
  135.4 1.0 copy-start.4
  136.5 0.7 copy-start.8
  190.7 6.9 %copy-start.16 = (f32[256,512]{1,0:T(8,128)S(1)}, f32[256,512]{1,0:T(8,128)}, u32[]{:S(2)}) copy-start(f32[256,512]{1,0:T(8,128)} %param.15) | copy-start | bytes 1572868
  191.8 16.2 %all-to-all-start.4 = ((f32[32,4,512]{2,1,0:T(4,128)}), f32[32,4,512]{2,1,0:T(4,128)S(1)}, u32[]{:S(2)}, u32[]{:S(2)}) async-start(f32[32,4,512]{2,1,0:T(4,128)} %copy.25), calls=%async_computation.4 | async-start | bytes 524288 | tf_op jit(solution)/shard_map/all_to_all | solution.py:345
  220.1 1.4 copy-start.19
